TPU v7x, 256 devices: a whole 4x4x8 slice. The times are simulated.
256 devices in a mesh: grp: 8 (over x_hi, y), tp: 32 (over x_lo, z, core).
Axes of the slice: x: 4 (x_hi: 2, x_lo: 2; x = x_hi * 2 + x_lo), y: 4, z: 8, core: 2. Of those that a mesh axis runs over, the one named last changes fastest.
Arguments:
- block_tokens: int32 [2560, 4], P('grp'), may hold values from 0 to 15999
- slot_of_row: int32 [2560], P('grp'), may hold values from 0 to 2559, as said below
- cache_lengths: int32 [2560], P('grp'), may hold values from 1 to 4
- embed_table: bfloat16 [16000, 2048], P('tp'), may hold values from -6 to 6
- norm_gain: float32 [8192], replicated, may hold values from 0.1 to 1.9
- query_weight: bfloat16 [8192, 4096], P(None, 'tp'), may hold values from -0.0625 to 0.0625
- key_value_weight: bfloat16 [2, 8192, 4096], P(None, None, 'tp'), may hold values from -0.0625 to 0.0625
- kv_cache: bfloat16 [2, 2560, 4, 4096], P(None, 'grp', None, 'tp'), may hold values from -730 to 730
- out_weight: bfloat16 [4096, 8192], P('tp'), may hold values from -0.1875 to 0.1875
- final_gain: float32 [8192], replicated, may hold values from 0.1 to 1.9
- prefix_weight: bfloat16 [8192, 4096], P(None, 'tp'), may hold values from -0.0625 to 0.0625
Outputs:
- prefix: bfloat16 [2560, 4096], P('grp', 'tp')
Inputs may be any that keep to these rules, and one draw needn't show every extreme that they name: `slot_of_row`: A permutation of all slots; slot s belongs to group s // 320. From the rows of one index of grp at most 80 go to one group, and in every draw some index of grp sends exactly 80 to some group.
All inputs are finite; a program needn't handle non-finite values.
Results may differ from a plain program's by a relative error of at most 0.027.
Values may be sent and summed in bfloat16 or wider, within the bound.
A program may use at most 128 MiB of HBM per device.

v0:
```python
import jax
import jax.numpy as jnp
from jax import lax
from jax.sharding import PartitionSpec as P

HEAD = 128
CACHE = 4


EPSILON = 1e-05


def rms_scale(rows, gain):
    values = rows.astype(jnp.float32)
    spread = jnp.mean(values * values, axis=-1, keepdims=True)
    return (values * lax.rsqrt(spread + EPSILON) * gain).astype(jnp.bfloat16)


def routing(slot_ids, owned, groups, capacity):
    target = slot_ids // owned
    place_in = slot_ids % owned
    member = (target[:, None] == jnp.arange(groups, dtype=jnp.int32)[None, :]).astype(jnp.int32)
    within = jnp.sum((jnp.cumsum(member, axis=0) - 1) * member, axis=1)
    return (target * capacity + within, place_in)


def pack_rows(values, slot_index, total):
    buffer = jnp.zeros((total,) + values.shape[1:], values.dtype)
    return buffer.at[slot_index].set(values)


def lookup_part(token_ids, table):
    vocab_rows = table.shape[0]
    local_ids = token_ids - lax.axis_index("tp") * vocab_rows
    inside = (local_ids >= 0) & (local_ids < vocab_rows)
    picked = jnp.take(table, jnp.clip(local_ids, 0, vocab_rows - 1), axis=0)
    picked = jnp.where(inside[..., None], picked, jnp.zeros_like(picked))
    return picked.reshape(token_ids.shape[0], -1).astype(jnp.float32)


def attend(normed, query_weight, key_value_weight, kv_cache, cache_lengths):
    row_count = normed.shape[0]
    queries = jnp.dot(normed, query_weight, preferred_element_type=jnp.float32).astype(jnp.bfloat16)
    fresh = jnp.einsum(
        "rg,kgd->krd", normed, key_value_weight, preferred_element_type=jnp.float32
    ).astype(jnp.bfloat16)
    heads_here = queries.shape[1] // HEAD
    query_heads = queries.reshape(row_count, heads_here, HEAD)
    key_heads = fresh[0].reshape(row_count, heads_here, HEAD)
    value_heads = fresh[1].reshape(row_count, heads_here, HEAD)
    cached = kv_cache.reshape(2, row_count, CACHE, heads_here, HEAD)
    scale = 1.0 / HEAD**0.5
    past = (
        jnp.einsum("rhd,rchd->rhc", query_heads, cached[0], preferred_element_type=jnp.float32)
        * scale
    )
    valid = jnp.arange(CACHE, dtype=jnp.int32)[None, None, :] < cache_lengths[:, None, None]
    past = jnp.where(valid, past, jnp.float32(-1e30))
    own_score = (
        jnp.sum(query_heads.astype(jnp.float32) * key_heads.astype(jnp.float32), axis=-1)[..., None]
        * scale
    )
    weights = jax.nn.softmax(jnp.concatenate([past, own_score], axis=-1), axis=-1).astype(
        jnp.bfloat16
    )
    mixed = jnp.einsum(
        "rhc,rchd->rhd", weights[..., :-1], cached[1], preferred_element_type=jnp.float32
    )
    mixed = mixed + weights[..., -1:].astype(jnp.float32) * value_heads.astype(jnp.float32)
    return mixed.reshape(row_count, -1).astype(jnp.bfloat16)


def shards(
    block_tokens,
    slot_of_row,
    cache_lengths,
    embed_table,
    norm_gain,
    query_weight,
    key_value_weight,
    kv_cache,
    out_weight,
    final_gain,
    prefix_weight,
):
    groups = lax.axis_size("grp")
    owned = slot_of_row.shape[0]
    capacity = 2 * owned // groups
    total = groups * capacity
    slot_index, place_in = routing(slot_of_row, owned, groups, capacity)
    sent_place = (
        jnp.full((total,), owned, jnp.int32).at[slot_index].set(place_in).reshape(groups, capacity)
    )
    shares = lax.psum_scatter(
        lookup_part(block_tokens, embed_table).astype(jnp.bfloat16),
        "tp",
        scatter_dimension=1,
        tiled=True,
    )
    sent_rows = pack_rows(shares, slot_index, total).reshape(groups, capacity, -1)
    got_rows, got_place = (
        lax.all_to_all(sent_rows, "grp", split_axis=0, concat_axis=0, tiled=True),
        lax.all_to_all(sent_place, "grp", split_axis=0, concat_axis=0, tiled=True),
    )
    got_place = got_place.reshape(total)
    own_part = (
        jnp.zeros((owned, shares.shape[1]), jnp.bfloat16)
        .at[got_place]
        .set(got_rows.reshape(total, -1), mode="drop")
    )
    whole = lax.all_gather(own_part, "tp", axis=1, tiled=True)
    normed = rms_scale(whole, norm_gain)
    attended = attend(normed, query_weight, key_value_weight, kv_cache, cache_lengths)
    partial_value = jnp.dot(attended, out_weight, preferred_element_type=jnp.float32)
    summed = lax.psum_scatter(
        partial_value.astype(jnp.bfloat16), "tp", scatter_dimension=1, tiled=True
    ).astype(jnp.float32)
    context = (own_part.astype(jnp.float32) + summed).astype(jnp.bfloat16)
    source_rows = jnp.minimum(got_place, owned - 1)
    back_rows = jnp.take(context, source_rows, axis=0).reshape(groups, capacity, -1)
    home_rows = lax.all_to_all(back_rows, "grp", split_axis=0, concat_axis=0, tiled=True).reshape(
        total, -1
    )
    mine = jnp.take(home_rows, slot_index, axis=0)
    full_rows = lax.all_gather(mine, "tp", axis=1, tiled=True)
    return jnp.dot(
        rms_scale(full_rows, final_gain), prefix_weight, preferred_element_type=jnp.float32
    ).astype(jnp.bfloat16)


def solution(mesh):
    in_specs = (
        P("grp", None),
        P("grp"),
        P("grp"),
        P("tp", None),
        P(),
        P(None, "tp"),
        P(None, None, "tp"),
        P(None, "grp", None, "tp"),
        P("tp", None),
        P(),
        P(None, "tp"),
    )
    out_specs = P("grp", "tp")
    return jax.shard_map(shards, mesh=mesh, in_specs=in_specs, out_specs=out_specs, check_vma=False)
```

profile of v0, /device:TPU:1, one launch (start us, length us, event | category | flops | bytes accessed | tf_op | source)
XLA Modules:
  0.0 508.3 jit_solution(15505839104722798762)
XLA Ops:
  6.5 0.0 copy-start
  6.5 0.0 reduce-scatter.3.cloned.1.call-start
  6.5 0.9 compare_and_fusion
  7.4 0.1 copy.19
  7.5 0.1 reshape.335
  7.7 12.7 %gather_fusion = bf16[1280,2048]{1,0:T(8,128)(2,1)} fusion(bf16[500,2048]{1,0:T(8,128)(2,1)} %param.14, s32[2048]{0:T(1024)S(1)} %pad_clamp_fusion), kind=kCustom, calls=%fused_computation | custom fusion | bytes 10490880 | tf_op jit(solution)/shard_map/jit(_take)/gather | solution.py:36
  20.4 8.7 %reshape.334 = bf16[320,4,2048]{2,1,0:T(4,128)(2,1)} reshape(bf16[1280,2048]{1,0:T(8,128)(2,1)} %gather_fusion) | data formatting | bytes 10485760 | tf_op jit(solution)/shard_map/jit(_take)/gather | solution.py:36
  29.0 0.2 copy.17
  29.2 0.2 copy.18
  29.4 5.8 %select_select_fusion = bf16[320,4,2048]{2,1,0:T(4,128)(2,1)S(1)} fusion(bf16[320,4,2048]{2,1,0:T(4,128)(2,1)} %reshape.334, pred[320,4]{1,0:T(8,128)(4,1)S(1)} %copy.18, pred[320,4]{1,0:T(8,128)(4,1)S(1)} %copy.17), kind=kLoop, calls=%fused_computation.22 | loop fusion | flops 5242880 | bytes 10488320 | tf_op jit(solution)/shard_map/jit(_where)/select_n | solution.py:37
  35.2 8.3 %copy.24 = bf16[40,8,4,2048]{3,1,2,0:T(8,128)(2,1)} copy(bf16[40,8,4,2048]{3,2,1,0:T(4,128)(2,1)S(1)} %bitcast.62) | data formatting | bytes 10485760
  43.6 0.0 reduce-scatter.3.cloned.1.call-update
  43.6 0.7 copy-done.4
  44.3 0.9 reduce-window.6
  45.1 0.2 slice_reduce_fusion
  45.4 0.1 add_bitcast_fusion
  45.5 2.9 scatter_custom_fusion
  48.4 0.7 all_to_all.12
  49.1 7.5 %all-to-all-start = ((s32[8,1,80]{2,1,0:T(1,128)}), s32[8,1,80]{2,1,0:T(1,128)S(1)}, u32[]{:S(2)}, u32[]{:S(2)}) async-start(s32[8,1,80]{2,1,0:T(1,128)} %all_to_all.12), calls=%async_computation | async-start | bytes 8192 | tf_op jit(solution)/shard_map/all_to_all | solution.py:103
  56.6 111.2 %reduce-scatter.3.cloned.1.call-done = bf16[320,256]{1,0:T(8,128)(2,1)} async-done(((bf16[320,8192]{1,0:T(8,128)(2,1)}), bf16[320,256]{1,0:T(8,128)(2,1)}) %reduce-scatter.3.cloned.1.call-update) | async-done | bytes 163856 | tf_op jit(solution)/shard_map/reduce_scatter | solution.py:94
  167.8 2.7 scatter_custom_fusion.1
  170.5 0.0 all-to-all-done
  170.5 5.9 %all-to-all-start.1 = ((bf16[8,80,256]{2,1,0:T(8,128)(2,1)}), bf16[8,80,256]{2,1,0:T(8,128)(2,1)S(1)}, u32[]{:S(2)}, u32[]{:S(2)}) async-start(bf16[8,80,256]{2,1,0:T(8,128)(2,1)} %bitcast.4), calls=%async_computation.2 | async-start | bytes 655360 | tf_op jit(solution)/shard_map/all_to_all | solution.py:102
  176.4 0.0 all-gather.3.cloned.1.call-start
  176.4 0.5 broadcast.247
  176.9 0.7 broadcast_minimum_fusion
  177.6 0.1 reshape.322
  177.7 6.5 %all-to-all-done.1 = bf16[8,80,256]{2,1,0:T(8,128)(2,1)S(1)} async-done(((bf16[8,80,256]{2,1,0:T(8,128)(2,1)}), bf16[8,80,256]{2,1,0:T(8,128)(2,1)S(1)}, u32[]{:S(2)}, u32[]{:S(2)}) %all-to-all-start.1) | async-done | bytes 327712 | tf_op jit(solution)/shard_map/all_to_all | solution.py:102
  184.2 5.9 %scatter_custom_fusion.2 = bf16[320,256]{1,0:T(8,128)(2,1)} fusion(s32[640]{0:T(1024)S(1)} %get-tuple-element.6, bf16[640,256]{1,0:T(8,128)(2,1)S(1)} %bitcast.65, bf16[]{:T(256)} %constant.63.clone.1), kind=kCustom, calls=%fused_computation.46 | custom fusion | bytes 163842 | tf_op jit(solution)/shard_map/scatter | solution.py:109
  190.2 0.0 all-gather.3.cloned.1.call-update
  190.2 0.0 reduce-scatter.5.cloned.1.call-start
  190.2 74.3 %all-gather.3.cloned.1.call-done = bf16[320,8192]{1,0:T(8,128)(2,1)} async-done(((bf16[320,256]{1,0:T(8,128)(2,1)}), bf16[320,8192]{1,0:T(8,128)(2,1)}) %all-gather.3.cloned.1.call-update) | async-done | bytes 5242896 | tf_op jit(solution)/shard_map/all_gather | solution.py:111
  264.6 3.8 fusion
  268.4 0.0 copy-done.8
  268.4 0.3 copy-done.1
  268.6 4.0 fusion.18
  272.6 0.0 copy-done.6
  272.6 0.0 copy-start.7
  272.6 0.0 copy-start.5
  272.6 1.7 fusion.31
  274.4 0.0 copy-done.7
  274.4 0.5 fusion.27
  274.9 0.1 copy.21
  275.0 0.0 copy-done.5
  275.1 0.2 copy.22
  275.3 0.5 fusion.28
  275.8 3.9 convolution_convert_fusion
  279.7 0.0 reduce-scatter.5.cloned.1.call-update
  279.8 118.2 %reduce-scatter.5.cloned.1.call-done = bf16[320,256]{1,0:T(8,128)(2,1)} async-done(((bf16[320,8192]{1,0:T(8,128)(2,1)}), bf16[320,256]{1,0:T(8,128)(2,1)}) %reduce-scatter.5.cloned.1.call-update) | async-done | bytes 163856 | tf_op jit(solution)/shard_map/reduce_scatter | solution.py:115
  398.0 1.0 add_convert_fusion
  398.9 0.0 copy-start.9
  398.9 2.8 gather_fusion.1
  401.7 0.9 broadcast_select_fusion
  402.6 6.4 %all-to-all-start.2 = ((bf16[8,80,256]{2,1,0:T(8,128)(2,1)}), bf16[8,80,256]{2,1,0:T(8,128)(2,1)S(1)}, u32[]{:S(2)}, u32[]{:S(2)}) async-start(bf16[8,80,256]{2,1,0:T(8,128)(2,1)} %broadcast_select_fusion), calls=%async_computation.4 | async-start | bytes 655360 | tf_op jit(solution)/shard_map/all_to_all | solution.py:121
  409.0 0.0 all-gather.5.cloned.1.call-start
  409.0 7.8 %all-to-all-done.2 = bf16[8,80,256]{2,1,0:T(8,128)(2,1)S(1)} async-done(((bf16[8,80,256]{2,1,0:T(8,128)(2,1)}), bf16[8,80,256]{2,1,0:T(8,128)(2,1)S(1)}, u32[]{:S(2)}, u32[]{:S(2)}) %all-to-all-start.2) | async-done | bytes 327712 | tf_op jit(solution)/shard_map/all_to_all | solution.py:121
  416.8 2.0 gather_fusion.2
  418.8 0.8 broadcast_select_fusion.1
  419.6 0.0 all-gather.5.cloned.1.call-update
  419.6 74.2 %all-gather.5.cloned.1.call-done = bf16[320,8192]{1,0:T(8,128)(2,1)} async-done(((bf16[320,256]{1,0:T(8,128)(2,1)}), bf16[320,8192]{1,0:T(8,128)(2,1)}) %all-gather.5.cloned.1.call-update) | async-done | bytes 5242896 | tf_op jit(solution)/shard_map/all_gather | solution.py:125
  493.9 3.8 fusion.3
  497.7 0.0 copy-done.9
  497.7 0.3 copy-done.2
  497.9 3.8 fusion.24
  (28 shorter events, 0.3 us)
Async XLA Ops:
  6.5 269.3 %copy-start = (bf16[128,8192]{1,0:T(8,128)(2,1)S(1)}, bf16[128,8192]{1,0:T(8,128)(2,1)}, u32[]{:S(2)}) copy-start(bf16[128,8192]{1,0:T(8,128)(2,1)} %param.19) | copy-start | bytes 6291460
  6.5 161.2 %reduce-scatter.3.cloned.1.call-start = ((), (), s32[]{:S(2)}) async-start(), calls=%async_computation.5 | async-start | bytes 5406720 | tf_op jit(solution)/shard_map/reduce_scatter | solution.py:94
  43.6 0.7 copy-start.4
  43.6 224.8 %copy-start.8 = (f32[8192]{0:T(1024)S(1)}, f32[8192]{0:T(1024)}, u32[]{:S(2)}) copy-start(f32[8192]{0:T(1024)} %param.15) | copy-start | bytes 98308
  49.1 121.4 %all-to-all-start = ((s32[8,1,80]{2,1,0:T(1,128)}), s32[8,1,80]{2,1,0:T(1,128)S(1)}, u32[]{:S(2)}, u32[]{:S(2)}) async-start(s32[8,1,80]{2,1,0:T(1,128)} %all_to_all.12), calls=%async_computation | async-start | bytes 8192 | tf_op jit(solution)/shard_map/all_to_all | solution.py:103
  170.5 13.7 %all-to-all-start.1 = ((bf16[8,80,256]{2,1,0:T(8,128)(2,1)}), bf16[8,80,256]{2,1,0:T(8,128)(2,1)S(1)}, u32[]{:S(2)}, u32[]{:S(2)}) async-start(bf16[8,80,256]{2,1,0:T(8,128)(2,1)} %bitcast.4), calls=%async_computation.2 | async-start | bytes 655360 | tf_op jit(solution)/shard_map/all_to_all | solution.py:102
  176.4 88.2 %all-gather.3.cloned.1.call-start = ((), (), s32[]{:S(2)}) async-start(), calls=%async_computation.6 | async-start | bytes 5406720 | tf_op jit(solution)/shard_map/all_gather | solution.py:111
  190.2 207.8 %reduce-scatter.5.cloned.1.call-start = ((), (), s32[]{:S(2)}) async-start(), calls=%async_computation.7 | async-start | bytes 5406720 | tf_op jit(solution)/shard_map/reduce_scatter | solution.py:115
  264.6 4.0 copy-start.1
  268.6 4.0 copy-start.6
  272.6 1.8 copy-start.7
  272.6 2.3 copy-start.5
  275.8 122.2 %copy-start.3 = (bf16[320,256]{1,0:T(8,128)(2,1)S(1)}, bf16[320,256]{1,0:T(8,128)(2,1)}, u32[]{:S(2)}) copy-start(bf16[320,256]{1,0:T(8,128)(2,1)} %scatter_custom_fusion.2) | copy-start | bytes 491524
  398.9 98.7 %copy-start.9 = (f32[8192]{0:T(1024)S(1)}, f32[8192]{0:T(1024)}, u32[]{:S(2)}) copy-start(f32[8192]{0:T(1024)} %param.20) | copy-start | bytes 98308
  402.6 14.2 %all-to-all-start.2 = ((bf16[8,80,256]{2,1,0:T(8,128)(2,1)}), bf16[8,80,256]{2,1,0:T(8,128)(2,1)S(1)}, u32[]{:S(2)}, u32[]{:S(2)}) async-start(bf16[8,80,256]{2,1,0:T(8,128)(2,1)} %broadcast_select_fusion), calls=%async_computation.4 | async-start | bytes 655360 | tf_op jit(solution)/shard_map/all_to_all | solution.py:121
  409.0 84.9 %all-gather.5.cloned.1.call-start = ((), (), s32[]{:S(2)}) async-start(), calls=%async_computation.8 | async-start | bytes 5406720 | tf_op jit(solution)/shard_map/all_gather | solution.py:125
  493.9 4.0 copy-start.2
Sparse Core Ops, SparseCore 0:
  43.7 124.0 reduce-scatter.2
  190.3 74.2 all-gather.2
  279.8 118.0 reduce-scatter.4
  419.8 74.0 all-gather.4
where the time goes:
time: 509 us; the launch traced here: 508 us
  waiting for transfers between devices  392 us (77%)
  local copies, waits for them, and re-layouts  49.7 us (10%)
  starting transfers between devices  19.8 us (4%)
  other arithmetic  18.7 us (4%)
  matrix products  14.4 us (3%)
  between operations  13.4 us (3%)
    reduce_scatter x1, waiting for transfers between devices, shards(): lax.psum_scatter(partial_value.astype(jnp.bfloat16), 'tp', scatter_dimens...  118 us
    reduce_scatter x1, waiting for transfers between devices, shards(): lax.psum_scatter(lookup_part(block_tokens, embed_table).astype(jnp.bfloat...  111 us
    all_gather x1, waiting for transfers between devices, shards(): whole = lax.all_gather(own_part, 'tp', axis=1, tiled=True)  74.3 us
    all_gather x1, waiting for transfers between devices, shards(): full_rows = lax.all_gather(mine, 'tp', axis=1, tiled=True)  74.2 us
    gather x2, local copies, waits for them, and re-layouts, lookup_part(): picked = jnp.take(table, jnp.clip(local_ids, 0, vocab_rows - 1), axis=0)  21.4 us
  transfers between devices with their start and end apart: 7, of which 6 were waited for; matrix products, arithmetic and copies ran while one was open for 2% of the time, Pallas kernels for 0%

commit v1 on v0

v1 whole, which is shorter than its diff:
```python
import functools

import jax
import jax.numpy as jnp
from jax import lax
from jax.experimental import pallas as pl
from jax.experimental.pallas import tpu as pltpu
from jax.sharding import PartitionSpec as P

MESH = pl.DeviceIdType.MESH
BF = jnp.bfloat16
F32 = jnp.float32
EPSILON = 1e-05
HEAD = 128
CACHE = 4
GROUPS = 8
RING = 8
OWN = 320
HALF = 160
QUART = 80
CAP = 80
LANES = 384
WIDE = 256
CHUNKS = 32
MINE = 16
VOCAB_ROWS = 500
SEMS = 192


def dot(a, b):
    return jnp.dot(a, b, preferred_element_type=F32)


def dot_lanes(a, b):
    return lax.dot_general(a, b, (((1,), (1,)), ((), ())), preferred_element_type=F32)


def ring_order(i):
    step = (i + 1) // 2
    return 4 + step * (1 - 2 * (i % 2))


class Wire:
    def __init__(self, send_sem, recv_sem):
        self.send_sem, self.recv_sem = send_sem, recv_sem
        self.used = 0
        self.sent = []

    def block(self, count):
        first = self.used
        self.used += count
        assert self.used <= SEMS
        return first

    def make(self, src, dst, peer, index):
        return pltpu.make_async_remote_copy(
            src_ref=src,
            dst_ref=dst,
            send_sem=self.send_sem.at[index],
            recv_sem=self.recv_sem.at[index],
            device_id=peer,
            device_id_type=MESH,
        )

    def send(self, src, dst, peer):
        copy = self.make(src, dst, peer, self.block(1))
        copy.start()
        self.sent.append(copy)
        return copy


def sum_and_share(wire, here, make, part, xland, lx, lz, zx, full, residual):
    core, xl, z, zp, zm, xm, cp = here
    base = core * MINE

    def zat(d):
        return lax.rem(z + (d + RING), RING)

    def x_copy(i, first):
        f = (1 - xl) * RING + lax.rem(z + ring_order(i), RING)
        return wire.make(part.at[f, pl.ds(0, HALF)], xland.at[i], xm, first + i)

    first_x = wire.block(RING)

    def x_step(i, carry):
        make((1 - xl) * RING + lax.rem(z + ring_order(i), RING), 0)
        x_copy(i, first_x).start()
        return carry

    lax.fori_loop(0, RING, x_step, 0)

    def z_step(i, carry):
        zz = lax.rem(z + ring_order(i), RING)
        make(2 * zz, 1)
        make(2 * zz + 1, 1)
        return carry

    z_step(0, 0)
    rx = [[None] * 4, [None] * 4]
    rz = [[None] * 4, [None] * 4]
    zrows = [(HALF, QUART), (HALF + QUART, QUART)]
    xrows = [(0, QUART), (QUART, QUART)]
    far = zat(4)
    for way, peer in ((0, zp), (1, zm)):
        lo, n = zrows[way]
        rz[way][0] = wire.send(
            part.at[pl.ds(2 * far, 2), pl.ds(lo, n)],
            lz.at[way, 0, :, pl.ds(lo - HALF, n)],
            peer,
        )
    lax.fori_loop(1, RING, z_step, 0)

    def own_step(i, carry):
        make(xl * RING + lax.rem(z + ring_order(i), RING), 0)
        return carry

    lax.fori_loop(0, RING, own_step, 0)

    def wait_x(i):
        x_copy(i, first_x).wait_recv()

    for k in range(4):
        for way, peer in ((0, zp), (1, zm)):
            zz = zat(4 - k if way == 0 else k - 4)
            f = xl * RING + zz
            if k == 0:
                if way == 0:
                    wait_x(0)
                    part[f, 0:HALF] = (
                        part[f, 0:HALF].astype(F32) + xland[0].astype(F32)
                    ).astype(BF)
                lo, n = xrows[way]
            else:
                i = 2 * k - 1 + way
                wait_x(i)
                rx[way][k - 1].wait_recv()
                for at, (slo, sn) in enumerate(xrows):
                    value = part[f, slo : slo + sn].astype(F32) + xland[i, slo : slo + sn].astype(F32)
                    if k > 1 or at == way:
                        value = value + lx[way, k - 1, slo : slo + sn].astype(F32)
                    part[f, slo : slo + sn] = value.astype(BF)
                lo, n = 0, HALF
            rx[way][k] = wire.send(
                part.at[f, pl.ds(lo, n)], lx.at[way, k, pl.ds(lo, n)], peer
            )
        if k > 0:
            for way, peer in ((0, zp), (1, zm)):
                zz = zat(4 - k if way == 0 else k - 4)
                rz[way][k - 1].wait_recv()
                lo, n = zrows[way] if k == 1 else (HALF, HALF)
                for e in range(2):
                    value = part[2 * zz + e, lo : lo + n].astype(F32)
                    value = value + lz[way, k - 1, e, lo - HALF : lo - HALF + n].astype(F32)
                    part[2 * zz + e, lo : lo + n] = value.astype(BF)
                rz[way][k] = wire.send(
                    part.at[pl.ds(2 * zz, 2), pl.ds(HALF, HALF)], lz.at[way, k], peer
                )

    rz[0][3].wait_recv()
    rz[1][3].wait_recv()

    def z_sum(e):
        return (
            part[2 * z + e, HALF:OWN].astype(F32)
            + lz[0, 3, e].astype(F32)
            + lz[1, 3, e].astype(F32)
        )

    part[2 * z + (1 - xl), HALF:OWN] = z_sum(1 - xl).astype(BF)
    cross = wire.send(part.at[2 * z + (1 - xl), pl.ds(HALF, HALF)], zx, xm)

    wait_x(7)
    rx[0][3].wait_recv()
    rx[1][3].wait_recv()
    f0 = xl * RING + z
    value = part[f0, 0:HALF].astype(F32) + xland[7].astype(F32)
    value = value + lx[0, 3].astype(F32) + lx[1, 3].astype(F32)
    if residual is not None:
        value = value + residual[base + f0, 0:HALF].astype(F32)
    full[base + f0, 0:HALF] = value.astype(BF)

    def xs(zz, lo=0, n=HALF, side=None):
        column = xl if side is None else side
        return full.at[base + column * RING + zz, pl.ds(lo, n)]

    def zs(zz, lo=HALF, n=HALF):
        return full.at[pl.ds(base + 2 * zz, 2), pl.ds(lo, n)]

    def go(ref, peer):
        return wire.send(ref, ref, peer)

    gx = [[go(xs(z), zp)], [go(xs(z), zm)]]
    gxx = [go(xs(z), xm)]
    gc = [go(xs(z), cp)]

    cross.wait_recv()
    value = z_sum(xl) + zx[...].astype(F32)
    mine = 2 * z + xl
    if residual is not None:
        value = value + residual[base + mine, HALF:OWN].astype(F32)
    full[base + mine, HALF:OWN] = value.astype(BF)
    swap = go(full.at[base + mine, pl.ds(HALF, HALF)], xm)
    swap.wait_recv()
    gz = [[go(zs(z), zp)], [go(zs(z), zm)]]
    gc.append(go(zs(z), cp))

    for k in range(1, 5):
        for way, peer in ((0, zp), (1, zm)):
            zz = zat(-k if way == 0 else k)
            gx[way][k - 1].wait_recv()
            if k < 4:
                lo, n = (0, HALF) if k < 3 else xrows[way]
                gx[way].append(go(xs(zz, lo, n), peer))
                gxx.append(go(xs(zz), xm))
                gc.append(go(xs(zz), cp))
        if k == 4:
            gxx.append(go(xs(zat(4)), xm))
            gc.append(go(xs(zat(4)), cp))
        for way, peer in ((0, zp), (1, zm)):
            zz = zat(-k if way == 0 else k)
            gz[way][k - 1].wait_recv()
            if k < 4:
                lo, n = (HALF, HALF) if k < 3 else zrows[way]
                gz[way].append(go(zs(zz, lo, n), peer))
                gc.append(go(zs(zz), cp))
        if k == 4:
            gc.append(go(zs(zat(4)), cp))
        for i in [0] if k == 1 else [2 * k - 3, 2 * k - 2]:
            gxx[i].wait_recv()
            d = (i + 1) // 2 if i % 2 == 0 else -((i + 1) // 2)
            gc.append(go(xs(zat(d), side=1 - xl), cp))
    gxx[7].wait_recv()
    gc.append(go(xs(zat(4), side=1 - xl), cp))
    for copy in gc:
        copy.wait_recv()

    def x_done(i, carry):
        x_copy(i, first_x).wait_send()
        return carry

    lax.fori_loop(0, RING, x_done, 0)


def project(full, gain_ref, weight, acc, squares):
    acc[...] = jnp.zeros_like(acc)
    squares[...] = jnp.zeros_like(squares)
    per = 4

    def step(s, carry):
        total, sq = None, None
        for e in range(per):
            i = s * per + e
            value = full[i].astype(F32)
            term = dot(
                (value * gain_ref[pl.ds(i, 1), :]).astype(BF),
                weight[pl.ds(pl.multiple_of(i * WIDE, WIDE), WIDE), :],
            )
            total = term if total is None else total + term
            sq = value * value if sq is None else sq + value * value
        acc[...] += total
        squares[...] += sq
        return carry

    lax.fori_loop(0, CHUNKS // per, step, 0)
    mean = jnp.sum(squares[...], axis=1, keepdims=True) * (1.0 / (CHUNKS * WIDE))
    return lax.rsqrt(mean + EPSILON)


def kernel(
    info_ref, lens_ref, gain_ref, final_ref, cache_ref, table_ref, wq_ref, wkv_ref, wo_ref, wp_ref,
    out_ref,
    info, tabs, wqkv, wo, wp, member, pack, unpack, onehot, part1, part2, xland1, xland2, lx1, lx2,
    lz1, lz2, zx1, zx2, full1, full2, att, acc, acc2, squares, outgo, back, local_sem, send_sem,
    recv_sem,
):
    g = lax.axis_index("grp")
    t = lax.axis_index("tp")
    core = t % 2
    z = (t // 2) % RING
    xl = t // (2 * RING)

    def place(x, zz, cc):
        return (g, (x * RING + zz) * 2 + cc)

    zp = place(xl, lax.rem(z + 1, RING), core)
    zm = place(xl, lax.rem(z + RING - 1, RING), core)
    xm = place(1 - xl, z, core)
    cp = place(xl, z, 1 - core)
    here = (core, xl, z, zp, zm, xm, cp)
    mates = [(lax.rem(g + k, GROUPS), t) for k in range(1, GROUPS)]

    loads = [
        pltpu.make_async_copy(table_ref, tabs.at[core], local_sem.at[0]),
        pltpu.make_async_copy(wq_ref, wqkv.at[:, pl.ds(0, HEAD)], local_sem.at[1]),
        pltpu.make_async_copy(wkv_ref.at[0], wqkv.at[:, pl.ds(HEAD, HEAD)], local_sem.at[2]),
        pltpu.make_async_copy(wkv_ref.at[1], wqkv.at[:, pl.ds(2 * HEAD, HEAD)], local_sem.at[3]),
        pltpu.make_async_copy(
            wo_ref.at[:, pl.ds(pl.multiple_of(core * MINE * WIDE, WIDE), MINE * WIDE)],
            wo.at[pl.ds(pl.multiple_of(core * HEAD, HEAD), HEAD)],
            local_sem.at[4],
        ),
        pltpu.make_async_copy(wp_ref, wp, local_sem.at[5]),
    ]
    for load in loads:
        load.start()
    info[g] = info_ref[...]

    barrier = pltpu.get_barrier_semaphore()
    peers = [zp, zm, xm, cp] + mates
    for peer in peers:
        pl.semaphore_signal(barrier, inc=1, device_id=peer, device_id_type=MESH)
    pl.semaphore_wait(barrier, len(peers))

    wire = Wire(send_sem, recv_sem)
    told = [wire.send(info.at[g], info.at[g], mate) for mate in mates]
    table_in = wire.send(table_ref, tabs.at[core], cp)
    wo_in = wire.send(
        wo_ref.at[:, pl.ds(pl.multiple_of((1 - core) * MINE * WIDE, WIDE), MINE * WIDE)],
        wo.at[pl.ds(pl.multiple_of(core * HEAD, HEAD), HEAD)],
        cp,
    )
    for copy in told:
        copy.wait_recv()

    slots = lax.broadcasted_iota(jnp.int32, (OWN, LANES), 0) + g * OWN
    codes = jnp.zeros((OWN, 8), F32)
    for e in range(GROUPS):
        hit = (info[e, 8:9, :] == slots).astype(F32).astype(BF)
        member[e] = hit
        codes = codes + dot_lanes(hit, info[e, 0:8, :].astype(F32).astype(BF))
    ids = codes[:, 0:4] * 128.0 + codes[:, 4:8]
    ids = jnp.where(core == 0, ids[:, 0:2], ids[:, 2:4]).astype(jnp.int32)
    ids = ids - (xl * RING + z) * (2 * VOCAB_ROWS)
    names = lax.broadcasted_iota(jnp.int32, (OWN, VOCAB_ROWS), 1)
    for j in range(2):
        for s in range(2):
            onehot[j, s] = (ids[:, j : j + 1] - s * VOCAB_ROWS == names).astype(F32).astype(BF)

    loads[0].wait()
    table_in.wait_recv()

    def embed(f, half):
        rows = pl.ds(half * HALF, HALF)
        j = f // 8
        columns = pl.ds(pl.multiple_of((f % 8) * WIDE, WIDE), WIDE)
        value = dot(onehot[j, 0, rows, :], tabs[0, :, columns])
        value = value + dot(onehot[j, 1, rows, :], tabs[1, :, columns])
        part1[f, rows, :] = value.astype(BF)

    sum_and_share(wire, here, embed, part1, xland1, lx1, lz1, zx1, full1, None)

    for load in loads[1:]:
        load.wait()
    scale = project(full1, gain_ref, wqkv, acc, squares)

    queries = (acc[:, 0:HEAD] * scale).astype(BF).astype(F32)
    keys = (acc[:, HEAD : 2 * HEAD] * scale).astype(BF).astype(F32)
    values = (acc[:, 2 * HEAD :] * scale).astype(BF).astype(F32)
    root = 1.0 / HEAD**0.5
    lens = lens_ref[...]
    scores = []
    for c in range(CACHE):
        s = jnp.sum(queries * cache_ref[0, c].astype(F32), axis=1, keepdims=True) * root
        scores.append(jnp.where(lens > c, s, -1e30))
    scores.append(jnp.sum(queries * keys, axis=1, keepdims=True) * root)
    top = functools.reduce(jnp.maximum, scores)
    raised = [jnp.exp(s - top) for s in scores]
    whole = functools.reduce(jnp.add, raised)
    weights = [(r / whole).astype(BF).astype(F32) for r in raised]
    mixed = weights[CACHE] * values
    for c in range(CACHE):
        mixed = mixed + weights[c] * cache_ref[1, c].astype(F32)
    att[core] = mixed.astype(BF)
    att_in = wire.send(att.at[core], att.at[core], cp)

    upper = (
        lax.broadcasted_iota(jnp.int32, (LANES, LANES), 0)
        <= lax.broadcasted_iota(jnp.int32, (LANES, LANES), 1)
    ).astype(F32).astype(BF)
    places = lax.broadcasted_iota(jnp.int32, (CAP, LANES), 0).astype(F32)
    own_slots = info[g, 8:9, :]
    for e in range(GROUPS):
        row = info[e, 8:9, :] - g * OWN
        inside = ((row >= 0) & (row < OWN)).astype(F32)
        rank = dot(inside.astype(BF), upper)
        pick = jnp.where(rank - 1.0 == places, inside, 0.0).astype(BF)
        pack[e] = dot_lanes(pick, member[e]).astype(BF)
        row = own_slots - e * OWN
        inside = ((row >= 0) & (row < OWN)).astype(F32)
        rank = dot(inside.astype(BF), upper)
        unpack[e] = jnp.where(rank - 1.0 == places, inside, 0.0).astype(BF)

    att_in.wait_recv()
    wo_in.wait_recv()

    def spread(f, half):
        rows = pl.ds(half * HALF, HALF)
        both = jnp.concatenate([att[0, rows, :], att[1, rows, :]], axis=1)
        columns = pl.ds(pl.multiple_of(f * WIDE, WIDE), WIDE)
        part2[f, rows, :] = dot(both, wo[:, columns]).astype(BF)

    sum_and_share(wire, here, spread, part2, xland2, lx2, lz2, zx2, full2, full1)

    scale = project(full2, final_ref, wp, acc2, squares)
    prefix = (acc2[...] * scale).astype(BF)
    homes = []
    for e in range(GROUPS):
        outgo[e] = dot(pack[e], prefix).astype(BF)
    for k, mate in enumerate(mates):
        homes.append(wire.send(outgo.at[mate[0]], back.at[g], mate))
    back[g] = outgo[g]
    for copy in homes:
        copy.wait_recv()
    result = jnp.zeros((LANES, HEAD), F32)
    for e in range(GROUPS):
        result = result + lax.dot_general(
            unpack[e], back[e], (((0,), (0,)), ((), ())), preferred_element_type=F32
        )
    out_ref[...] = result[0:OWN].astype(BF)
    for copy in wire.sent:
        copy.wait_send()


def shards(
    block_tokens, slot_of_row, cache_lengths, embed_table, norm_gain, query_weight, key_value_weight,
    kv_cache, out_weight, final_gain, prefix_weight,
):
    tokens = block_tokens.T
    info = jnp.concatenate([tokens >> 7, tokens & 127, slot_of_row[None, :]], axis=0)
    info = jnp.pad(info, ((0, 16 - 9), (0, LANES - OWN)), constant_values=-1)
    cache = kv_cache.reshape(2, OWN, CACHE, HEAD).transpose(0, 2, 1, 3)
    vmem = pl.BlockSpec(memory_space=pltpu.VMEM)
    hbm = pl.BlockSpec(memory_space=pl.ANY)
    return pl.pallas_call(
        kernel,
        out_shape=jax.ShapeDtypeStruct((OWN, HEAD), BF),
        in_specs=[vmem] * 5 + [hbm] * 5,
        out_specs=vmem,
        scratch_shapes=[
            pltpu.VMEM((GROUPS, 16, LANES), jnp.int32),
            pltpu.VMEM((2, VOCAB_ROWS, 2048), BF),
            pltpu.VMEM((CHUNKS * WIDE, 3 * HEAD), BF),
            pltpu.VMEM((2 * HEAD, MINE * WIDE), BF),
            pltpu.VMEM((CHUNKS * WIDE, HEAD), BF),
            pltpu.VMEM((GROUPS, OWN, LANES), BF),
            pltpu.VMEM((GROUPS, CAP, OWN), BF),
            pltpu.VMEM((GROUPS, CAP, LANES), BF),
            pltpu.VMEM((2, 2, OWN, VOCAB_ROWS), BF),
        ]
        + [pltpu.VMEM((MINE, OWN, WIDE), BF)] * 2
        + [pltpu.VMEM((RING, HALF, WIDE), BF)] * 2
        + [pltpu.VMEM((2, 4, HALF, WIDE), BF)] * 2
        + [pltpu.VMEM((2, 4, 2, HALF, WIDE), BF)] * 2
        + [pltpu.VMEM((HALF, WIDE), BF)] * 2
        + [pltpu.VMEM((CHUNKS, OWN, WIDE), BF)] * 2
        + [
            pltpu.VMEM((2, OWN, HEAD), BF),
            pltpu.VMEM((OWN, 3 * HEAD), F32),
            pltpu.VMEM((OWN, HEAD), F32),
            pltpu.VMEM((OWN, WIDE), F32),
            pltpu.VMEM((GROUPS, CAP, HEAD), BF),
            pltpu.VMEM((GROUPS, CAP, HEAD), BF),
            pltpu.SemaphoreType.DMA((6,)),
            pltpu.SemaphoreType.DMA((SEMS,)),
            pltpu.SemaphoreType.DMA((SEMS,)),
        ],
        compiler_params=pltpu.CompilerParams(
            collective_id=0, has_side_effects=True, vmem_limit_bytes=56 * 1024 * 1024
        ),
    )(
        info,
        cache_lengths[:, None],
        norm_gain.reshape(CHUNKS, WIDE),
        final_gain.reshape(CHUNKS, WIDE),
        cache,
        embed_table,
        query_weight,
        key_value_weight,
        out_weight,
        prefix_weight,
    )


def solution(mesh):
    in_specs = (
        P("grp", None),
        P("grp"),
        P("grp"),
        P("tp", None),
        P(),
        P(None, "tp"),
        P(None, None, "tp"),
        P(None, "grp", None, "tp"),
        P("tp", None),
        P(),
        P(None, "tp"),
    )
    return jax.shard_map(
        shards, mesh=mesh, in_specs=in_specs, out_specs=P("grp", "tp"), check_vma=False
    )
```

time: 509 us -> 163 us (0.32)
  waiting for transfers between devices: 392 us -> 0 us
  Pallas kernels: 0 us -> 153 us
  local copies, waits for them, and re-layouts: 49.7 us -> 9.03 us
  starting transfers between devices: 19.8 us -> 0 us
  other arithmetic: 18.7 us -> 0.71 us
  matrix products: 14.4 us -> 0 us
  between operations: 13.4 us -> 0.01 us
    reduce_scatter x2 -> x0, waiting for transfers between devices: 229 us -> none  [the longest x1 118 us: shards(): lax.psum_scatter(partial_value.astype(jnp.bfloat16), 'tp', scatter_dimens...]
    pallas_call x0 -> x1, Pallas kernels: none -> 153 us  [shards(): pl.pallas_call(kernel, out_shape=jax.ShapeDtypeStruct((OWN, HEAD), BF), i...]
    all_gather x2 -> x0, waiting for transfers between devices: 149 us -> none  [the longest x1 74.3 us: shards(): whole = lax.all_gather(own_part, 'tp', axis=1, tiled=True)]
    gather x4 -> x0, local copies, waits for them, and re-layouts: 26.1 us -> none  [the longest x2 21.4 us: lookup_part(): picked = jnp.take(table, jnp.clip(local_ids, 0, vocab_rows - 1), axis=0)]
    all_to_all x3 -> x0, starting transfers between devices: 19.7 us -> none  [the longest x1 7.48 us: shards(): lax.all_to_all(sent_place, 'grp', split_axis=0, concat_axis=0, tiled=True)]
    dot_general x6 -> x0, matrix products: 14.4 us -> none  [the longest x1 3.97 us: attend(): jnp.einsum('rg,kgd->krd', normed, key_value_weight, preferred_element_typ...]
    all_to_all x3 -> x0, waiting for transfers between devices: 14.3 us -> none  [the longest x1 7.78 us: shards(): lax.all_to_all(back_rows, 'grp', split_axis=0, concat_axis=0, tiled=True)]
    scatter x3 -> x0, local copies, waits for them, and re-layouts: 11.6 us -> none  [the longest x1 5.95 us: shards(): own_part = jnp.zeros((owned, shares.shape[1]), jnp.bfloat16).at[got_place...]
  transfers between devices with their start and end apart: 7 -> 0, of which waited for: 6 -> 0; matrix products, arithmetic and copies ran while one was open for 2% -> 0% of each run, Pallas kernels for 0% -> 0%
where the time goes in v1:
time: 163 us
  Pallas kernels  153 us (94%)
  local copies, waits for them, and re-layouts  9.03 us (6%)
    pallas_call x1, Pallas kernels, shards(): pl.pallas_call(kernel, out_shape=jax.ShapeDtypeStruct((OWN, HEAD), BF), i...  153 us
    unnamed x2, local copies, waits for them, and re-layouts  3.55 us

profile of v1, /device:TPU:1, one launch (start us, length us, event | category | flops | bytes accessed | tf_op | source)
XLA Modules:
  0.0 163.0 jit_solution(14912847493540421739)
XLA Ops:
  0.0 0.7 broadcast_in_dim.6
  0.7 0.7 shift-right-arithmetic_bitcast_fusion
  1.4 0.6 pad.4.info_ref
  2.0 1.4 reshape.6.gain_ref
  3.4 1.4 reshape.7.final_ref
  4.7 1.4 broadcast_in_dim.8.lens_ref
  6.2 2.0 %copy.16 = bf16[2,320,4,128]{3,1,2,0:T(8,128)(2,1)} copy(bf16[2,320,4,128]{3,2,1,0:T(4,128)(2,1)} %param.18) | data formatting | bytes 1310720 | tf_op args[7]
  8.2 153.3 %shard_map.109 = bf16[320,128]{1,0:T(8,128)(2,1)} custom-call(s32[16,384]{1,0:T(8,128)} %pad.4.info_ref, s32[320,1]{1,0:T(8,128)} %broadcast_in_dim.8.lens_ref, f32[32,256]{1,0:T(8,128)} %reshape.6.gain_ref, f32[32,256]{1,0:T(8,128)} %reshape.7.final_ref, bf16[2,4,320,128]{3,2,1,0:T(8,128)(2,1)} %bitcast.7, bf16[500,2048]{1,0:T(8,128)(2,1)} %table_ref.1, ...), custom_call_target="tpu_custom_call" | custom-call | tf_op jit(solution)/shard_map/pallas_call | solution.py:434
  161.5 1.5 copy.18
  (1 shorter events, 0.0 us)

commit v2 on v1

v2 whole, which is shorter than its diff:
```python
import functools

import jax
import jax.numpy as jnp
from jax import lax
from jax.experimental import pallas as pl
from jax.experimental.pallas import tpu as pltpu
from jax.sharding import PartitionSpec as P

MESH = pl.DeviceIdType.MESH
BF = jnp.bfloat16
F32 = jnp.float32
EPSILON = 1e-05
HEAD = 128
CACHE = 4
GROUPS = 8
RING = 8
OWN = 320
HALF = 160
QUART = 80
CAP = 80
LANES = 384
WIDE = 256
CHUNKS = 32
MINE = 16
VOCAB_ROWS = 500
SEMS = 224
QUAD = 4
SPAN = 2048


def dot(a, b):
    return jnp.dot(a, b, preferred_element_type=F32)


def dot_lanes(a, b):
    return lax.dot_general(a, b, (((1,), (1,)), ((), ())), preferred_element_type=F32)


def ring_order(i):
    step = (i + 1) // 2
    return 4 + step * (1 - 2 * (i % 2))


class Wire:
    def __init__(self, send_sem, recv_sem):
        self.send_sem, self.recv_sem = send_sem, recv_sem
        self.used = 0
        self.sent = []

    def block(self, count):
        first = self.used
        self.used += count
        assert self.used <= SEMS
        return first

    def make(self, src, dst, peer, index):
        return pltpu.make_async_remote_copy(
            src_ref=src,
            dst_ref=dst,
            send_sem=self.send_sem.at[index],
            recv_sem=self.recv_sem.at[index],
            device_id=peer,
            device_id_type=MESH,
        )

    def send(self, src, dst, peer):
        copy = self.make(src, dst, peer, self.block(1))
        copy.start()
        self.sent.append(copy)
        return copy


class Ring:
    def __init__(self, wire, here, part, land, streams):
        self.wire, self.here, self.part, self.land, self.streams = wire, here, part, land, streams
        self.got = [[[None] * 4, [None] * 4] for _ in streams]

    def zat(self, d):
        return lax.rem(self.here.z + (d + RING), RING)

    def push(self, s, way, k, f, lo, a, n):
        self.got[s][way][k] = self.wire.send(
            self.part.at[f, pl.ds(lo + a, n)],
            self.land.at[s, way, k, pl.ds(a, n)],
            self.here.zp if way == 0 else self.here.zm,
        )

    def hop0(self, s):
        index, lo, n, far, extra = self.streams[s]
        f = index(self.zat(4))
        if extra is not None:
            rows = slice(lo, lo + n)
            self.part[f, rows] = (self.part[f, rows].astype(F32) + extra(0)).astype(BF)
        for way in range(2):
            a, m = far[way]
            if m:
                self.push(s, way, 0, f, lo, a, m)

    def hop(self, k, s):
        index, lo, n, far, extra = self.streams[s]
        part = self.part
        for way in range(2):
            f = index(self.zat(4 - k if way == 0 else k - 4))
            a, m = far[way] if k == 1 else (0, n)
            if self.got[s][way][k - 1] is not None:
                self.got[s][way][k - 1].wait_recv()
            other = None if extra is None else extra(2 * k - 1 + way)
            cuts = sorted({0, a, a + m, n}) if m else [0, n]
            for lo2, hi2 in zip(cuts[:-1], cuts[1:]):
                landed = m > 0 and lo2 >= a and hi2 <= a + m
                if not landed and other is None:
                    continue
                rows = slice(lo + lo2, lo + hi2)
                value = part[f, rows].astype(F32)
                if other is not None:
                    value = value + other[lo2:hi2]
                if landed:
                    value = value + self.land[s, way, k - 1, lo2:hi2].astype(F32)
                part[f, rows] = value.astype(BF)
            self.push(s, way, k, f, lo, 0, n)

    def total(self, s):
        index, lo, n, far, extra = self.streams[s]
        self.got[s][0][3].wait_recv()
        self.got[s][1][3].wait_recv()
        value = self.part[index(self.here.z), lo : lo + n].astype(F32)
        value = value + self.land[s, 0, 3, 0:n].astype(F32) + self.land[s, 1, 3, 0:n].astype(F32)
        return value if extra is None else value + extra(7)


class Share:
    def __init__(self, wire, here, full, streams):
        self.wire, self.here, self.full, self.streams = wire, here, full, streams
        self.got = [[[], []] for _ in streams]

    def zat(self, d):
        return lax.rem(self.here.z + (d + RING), RING)

    def view(self, s, d, a=0, n=None):
        index, lo, rows, far, tap = self.streams[s]
        return self.full.at[index(self.zat(d)), pl.ds(lo + a, rows if n is None else n)]

    def push(self, s, way, d, a=0, n=None):
        ref = self.view(s, d, a, n)
        peer = self.here.zp if way == 0 else self.here.zm
        self.got[s][way].append(self.wire.send(ref, ref, peer))

    def begin(self, s):
        self.push(s, 0, 0)
        self.push(s, 1, 0)
        if self.streams[s][4] is not None:
            self.streams[s][4](s, 0)

    def hop(self, k, s):
        index, lo, n, far, tap = self.streams[s]
        for way in range(2):
            d = -k if way == 0 else k
            if k == 4:
                if far[way][1]:
                    self.got[s][way][3].wait_recv()
                continue
            self.got[s][way][k - 1].wait_recv()
            if k < 3:
                self.push(s, way, d)
            elif far[way][1]:
                self.push(s, way, d, *far[way])
            if tap is not None:
                tap(s, d)
        if k == 4 and tap is not None:
            tap(s, 4)


SPLIT = ((0, QUART), (QUART, QUART))
UP = ((0, QUART), (0, 0))
DOWN = ((0, 0), (0, QUART))


def sum_and_share(wire, here, make, part, xland, land, zx, full, tag=""):
    core, xl, z = here.core, here.xl, here.z
    base = core * MINE

    def x_copy(i, first):
        f = (1 - xl) * RING + lax.rem(z + ring_order(i), RING)
        return wire.make(part.at[f, pl.ds(0, HALF)], xland.at[i], here.xm, first + i)

    first_x = wire.block(RING)

    def x_step(i, carry):
        make((1 - xl) * RING + lax.rem(z + ring_order(i), RING), 0)
        x_copy(i, first_x).start()
        return carry

    lax.fori_loop(0, RING, x_step, 0)

    def z_step(i, carry):
        zz = lax.rem(z + ring_order(i), RING)
        make(2 * zz, 1)
        make(2 * zz + 1, 1)
        return carry

    def own_step(i, carry):
        make(xl * RING + lax.rem(z + ring_order(i), RING), 0)
        return carry

    def crossed(i):
        x_copy(i, first_x).wait_recv()
        return xland[i].astype(F32)

    streams = [
        (lambda zz: xl * RING + zz, 0, HALF, SPLIT, crossed),
        (lambda zz: 2 * zz + (1 - xl), HALF, HALF, SPLIT, None),
        (lambda zz: 2 * zz + xl, HALF, HALF, SPLIT, None),
    ]
    ring = Ring(wire, here, part, land, streams)
    z_step(0, 0)
    ring.hop0(1)
    ring.hop0(2)
    lax.fori_loop(1, RING, z_step, 0)
    lax.fori_loop(0, RING, own_step, 0)
    ring.hop0(0)
    for k in (1, 2, 3):
        for s in (1, 0, 2):
            ring.hop(k, s)
    away = 2 * z + (1 - xl)
    part[away, HALF:OWN] = ring.total(1).astype(BF)
    cross = wire.send(part.at[away, pl.ds(HALF, HALF)], zx, here.xm)
    full[base + xl * RING + z, 0:HALF] = ring.total(0).astype(BF)

    gxx, gc = {}, []

    def late(s, d):
        ref = share.view(s, d)
        gxx[d] = wire.send(ref, ref, here.xm)
        gc.append(wire.send(ref, ref, here.cp))

    def near(s, d):
        ref = share.view(s, d)
        gc.append(wire.send(ref, ref, here.cp))

    def beside(d):
        gxx[d].wait_recv()
        ref = full.at[base + (1 - xl) * RING + share.zat(d), pl.ds(0, HALF)]
        gc.append(wire.send(ref, ref, here.cp))

    share = Share(
        wire,
        here,
        full,
        [
            (lambda zz: base + xl * RING + zz, 0, HALF, SPLIT, late),
            (lambda zz: base + 2 * zz + xl, HALF, HALF, SPLIT, near),
            (lambda zz: base + 2 * zz + (1 - xl), HALF, HALF, SPLIT, near),
        ],
    )
    share.begin(0)
    value = ring.total(2)
    cross.wait_recv()
    full[base + 2 * z + xl, HALF:OWN] = (value + zx[...].astype(F32)).astype(BF)
    ref = share.view(1, 0)
    swap = wire.send(ref, ref, here.xm)
    share.begin(1)
    swap.wait_recv()
    share.begin(2)
    for k in (1, 2, 3, 4):
        for s in range(3):
            share.hop(k, s)
        for d in [0] if k == 1 else [1 - k, k - 1]:
            beside(d)
    beside(4)
    for copy in gc:
        copy.wait_recv()

    def x_done(i, carry):
        x_copy(i, first_x).wait_send()
        return carry

    lax.fori_loop(0, RING, x_done, 0)


def gain_row(gain_ref, i):
    return jnp.concatenate([gain_ref[pl.ds(2 * i, 1), :], gain_ref[pl.ds(2 * i + 1, 1), :]], axis=1)


def project(full, gain_ref, weight, acc, squares):
    acc[...] = jnp.zeros_like(acc)
    squares[...] = jnp.zeros_like(squares)
    per = 4

    def step(s, carry):
        total, sq = None, None
        for e in range(per):
            i = s * per + e
            value = full[i].astype(F32)
            term = dot(
                (value * gain_row(gain_ref, i)).astype(BF),
                weight[pl.ds(pl.multiple_of(i * WIDE, WIDE), WIDE), :],
            )
            total = term if total is None else total + term
            sq = value * value if sq is None else sq + value * value
        acc[...] += total
        squares[...] += sq
        return carry

    lax.fori_loop(0, CHUNKS // per, step, 0)
    mean = jnp.sum(squares[...], axis=1, keepdims=True) * (1.0 / (CHUNKS * WIDE))
    return lax.rsqrt(mean + EPSILON)


class Here:
    pass


def kernel(
    tokens_ref, slots_ref, lens_ref, gain_ref, final_ref, cache_ref, table_ref, wq_ref, wkv_ref, wo_ref,
    wp_ref, out_ref,
    info, tabs, wqkv, woq, wpq, member, pack, unpack, onehot, natural, cache, part1, part2, xland, land1,
    land2, zx, full1, full2, att, acc, acc4, squares, partial, outgo, back, local_sem, send_sem, recv_sem,
):
    g = lax.axis_index("grp")
    t = lax.axis_index("tp")
    here = Here()
    core = here.core = t % 2
    z = here.z = (t // 2) % RING
    xl = here.xl = t // (2 * RING)
    quarter = core * 2 + xl

    def place(x, zz, cc):
        return (x * RING + zz) * 2 + cc

    here.zp = (g, place(xl, lax.rem(z + 1, RING), core))
    here.zm = (g, place(xl, lax.rem(z + RING - 1, RING), core))
    here.xm = (g, place(1 - xl, z, core))
    here.cp = (g, place(xl, z, 1 - core))
    dg = (g, place(1 - xl, z, 1 - core))
    og = lax.rem(g + GROUPS // 2, GROUPS)
    xm_other = (og, here.xm[1])
    dg_other = (og, dg[1])
    cp_quarter = (1 - core) * 2 + xl
    xm_quarter = core * 2 + (1 - xl)
    dg_quarter = (1 - core) * 2 + (1 - xl)
    mates = [(lax.rem(g + k, GROUPS), t) for k in range(1, GROUPS)]

    def wide(i, n):
        return pl.ds(pl.multiple_of(i * n, n), n)

    table_load = pltpu.make_async_copy(table_ref, tabs.at[core], local_sem.at[0])
    loads = [
        pltpu.make_async_copy(cache_ref, natural, local_sem.at[6]),
        pltpu.make_async_copy(wq_ref, wqkv.at[:, pl.ds(0, HEAD)], local_sem.at[1]),
        pltpu.make_async_copy(wkv_ref.at[0], wqkv.at[:, pl.ds(HEAD, HEAD)], local_sem.at[2]),
        pltpu.make_async_copy(wkv_ref.at[1], wqkv.at[:, pl.ds(2 * HEAD, HEAD)], local_sem.at[3]),
        pltpu.make_async_copy(
            wo_ref.at[:, wide(quarter, SPAN)], woq.at[wide(quarter, HEAD)], local_sem.at[4]
        ),
        pltpu.make_async_copy(
            wp_ref.at[wide(quarter, SPAN)], wpq.at[:, wide(quarter, HEAD)], local_sem.at[5]
        ),
    ]
    table_load.start()
    info[g] = jnp.full((16, LANES), -1, jnp.int32)
    info[g, 0:4, 0:OWN] = tokens_ref[...]
    info[g, 8:9, 0:OWN] = slots_ref[...].reshape(1, OWN)

    barrier = pltpu.get_barrier_semaphore()
    peers = [here.zp, here.zm, here.xm, here.cp, dg, xm_other, dg_other] + mates
    for peer in peers:
        pl.semaphore_signal(barrier, inc=1, device_id=peer, device_id_type=MESH)
    pl.semaphore_wait(barrier, len(peers))

    wire = Wire(send_sem, recv_sem)
    told = [wire.send(info.at[g], info.at[g], mate) for mate in mates]
    table_in = wire.send(table_ref, tabs.at[core], here.cp)
    for load in loads:
        load.start()

    half = SPAN // 2

    def give_wo(who, q, lo, n):
        cols = pl.ds(pl.multiple_of(q * SPAN + lo, half), n)
        return wire.send(wo_ref.at[:, cols], woq.at[wide(quarter, HEAD), pl.ds(lo, n)], who)

    def give_wp(who, q, lo, n):
        rows = pl.ds(pl.multiple_of(q * SPAN + lo, half), n)
        return wire.send(wp_ref.at[rows], wpq.at[pl.ds(lo, n), wide(quarter, HEAD)], who)

    wo_in = [
        give_wo(here.cp, cp_quarter, 0, SPAN),
        give_wo(here.xm, xm_quarter, 0, half),
        give_wo(xm_other, xm_quarter, half, half),
        give_wo(dg, dg_quarter, 0, half),
        give_wo(dg_other, dg_quarter, half, half),
    ]
    for copy in told:
        copy.wait_recv()

    slots = lax.broadcasted_iota(jnp.int32, (OWN, LANES), 0) + g * OWN
    codes = jnp.zeros((OWN, 8), F32)
    for e in range(GROUPS):
        hit = (info[e, 8:9, :] == slots).astype(F32).astype(BF)
        member[e] = hit
        heard = info[e, 0:4, :]
        heard = jnp.concatenate([heard >> 7, heard & 127], axis=0)
        codes = codes + dot_lanes(hit, heard.astype(F32).astype(BF))
    ids = codes[:, 0:4] * 128.0 + codes[:, 4:8]
    ids = jnp.where(core == 0, ids[:, 0:2], ids[:, 2:4]).astype(jnp.int32)
    ids = ids - (xl * RING + z) * (2 * VOCAB_ROWS)
    names = lax.broadcasted_iota(jnp.int32, (OWN, VOCAB_ROWS), 1)
    for j in range(2):
        for s in range(2):
            onehot[j, s] = (ids[:, j : j + 1] - s * VOCAB_ROWS == names).astype(F32).astype(BF)

    table_load.wait()
    table_in.wait_recv()

    def embed(f, side):
        rows = pl.ds(side * HALF, HALF)
        j = f // 8
        columns = wide(f % 8, WIDE)
        value = dot(onehot[j, 0, rows, :], tabs[0, :, columns])
        value = value + dot(onehot[j, 1, rows, :], tabs[1, :, columns])
        part1[f, rows, :] = value.astype(BF)

    sum_and_share(wire, here, embed, part1, xland, land1, zx, full1)

    for load in loads:
        load.wait()
    for k in range(2):
        for b in range(4):
            rows = slice(b * 80, b * 80 + 80)
            block = natural[k, rows].astype(F32)
            for c in range(CACHE):
                cache[k, c, rows] = block[:, c, :].astype(BF)
    scale = project(full1, gain_ref, wqkv, acc, squares)

    queries = (acc[:, 0:HEAD] * scale).astype(BF).astype(F32)
    keys = (acc[:, HEAD : 2 * HEAD] * scale).astype(BF).astype(F32)
    values = (acc[:, 2 * HEAD :] * scale).astype(BF).astype(F32)
    root = 1.0 / HEAD**0.5
    diagonal = lax.broadcasted_iota(jnp.int32, (OWN, OWN), 0) == lax.broadcasted_iota(
        jnp.int32, (OWN, OWN), 1
    )
    lens = jnp.sum(
        jnp.where(diagonal, lens_ref[...].reshape(1, OWN).astype(F32), 0.0), axis=1, keepdims=True
    )
    scores = []
    for c in range(CACHE):
        s = jnp.sum(queries * cache[0, c].astype(F32), axis=1, keepdims=True) * root
        scores.append(jnp.where(lens > c + 0.5, s, -1e30))
    scores.append(jnp.sum(queries * keys, axis=1, keepdims=True) * root)
    top = functools.reduce(jnp.maximum, scores)
    raised = [jnp.exp(s - top) for s in scores]
    whole = functools.reduce(jnp.add, raised)
    weights = [(r / whole).astype(BF).astype(F32) for r in raised]
    mixed = weights[CACHE] * values
    for c in range(CACHE):
        mixed = mixed + weights[c] * cache[1, c].astype(F32)
    att[quarter] = mixed.astype(BF)
    att_in = [wire.send(att.at[quarter], att.at[quarter], who) for who in (here.xm, dg, here.cp)]

    upper = (
        lax.broadcasted_iota(jnp.int32, (LANES, LANES), 0)
        <= lax.broadcasted_iota(jnp.int32, (LANES, LANES), 1)
    ).astype(F32).astype(BF)
    places = lax.broadcasted_iota(jnp.int32, (CAP, LANES), 0).astype(F32)
    own_slots = info[g, 8:9, :]
    for e in range(GROUPS):
        row = info[e, 8:9, :] - g * OWN
        inside = ((row >= 0) & (row < OWN)).astype(F32)
        rank = dot(inside.astype(BF), upper)
        pick = jnp.where(rank - 1.0 == places, inside, 0.0).astype(BF)
        pack[e] = dot_lanes(pick, member[e]).astype(BF)
        row = own_slots - e * OWN
        inside = ((row >= 0) & (row < OWN)).astype(F32)
        rank = dot(inside.astype(BF), upper)
        unpack[e] = jnp.where(rank - 1.0 == places, inside, 0.0).astype(BF)

    for copy in att_in + wo_in:
        copy.wait_recv()
    wp_in = [
        give_wp(here.cp, cp_quarter, 0, SPAN),
        give_wp(here.xm, xm_quarter, 0, half),
        give_wp(xm_other, xm_quarter, half, half),
        give_wp(dg, dg_quarter, 0, half),
        give_wp(dg_other, dg_quarter, half, half),
    ]

    def spread(i, carry):
        zz = lax.rem(z + ring_order(i), RING)
        both = jnp.concatenate([att[q] for q in range(QUAD)], axis=1)
        part2[zz] = dot(both, woq[:, wide(zz, WIDE)]).astype(BF)
        return carry

    strips = [(lambda zz: zz, QUART * s, QUART, (UP, DOWN)[s % 2], None) for s in range(QUAD)]
    ring = Ring(wire, here, part2, land2, strips)
    spread(0, 0)
    for s in range(QUAD):
        ring.hop0(s)
    lax.fori_loop(1, RING, spread, 0)
    for k in (1, 2, 3):
        for s in range(QUAD):
            ring.hop(k, s)
    share = Share(wire, here, full2, strips)
    for s in range(QUAD):
        rows = slice(QUART * s, QUART * s + QUART)
        value = ring.total(s) + full1[quarter * RING + z, rows].astype(F32)
        full2[z, rows] = value.astype(BF)
        share.begin(s)

    def take(zz, first):
        value = full2[zz].astype(F32)
        scaled = (value * gain_row(final_ref, quarter * RING + zz)).astype(BF)
        term = dot(scaled, wpq[wide(zz, WIDE), :])
        if first:
            acc4[...] = term
            squares[...] = value * value
        else:
            acc4[...] += term
            squares[...] += value * value

    for copy in wp_in:
        copy.wait_recv()
    take(z, True)
    for k in (1, 2, 3, 4):
        for s in range(QUAD):
            share.hop(k, s)
        take(share.zat(-k), False)
        if k < 4:
            take(share.zat(k), False)

    square = jnp.sum(squares[...], axis=1, keepdims=True)
    high = square.astype(BF).astype(F32)
    lanes = lax.broadcasted_iota(jnp.int32, (OWN, HEAD), 1)
    tail = jnp.where(lanes < HEAD // 2, high, square - high).astype(BF)
    for q in range(QUAD):
        partial[q, 0] = acc4[:, q * HEAD : (q + 1) * HEAD].astype(BF)
        partial[q, 1] = tail
    sums = [
        wire.send(partial.at[q], back.at[quarter], who)
        for who, q in ((here.xm, xm_quarter), (dg, dg_quarter), (here.cp, cp_quarter))
    ]
    back[quarter] = partial[quarter]
    for copy in sums:
        copy.wait_recv()
    prefix, square = None, None
    for q in range(QUAD):
        term = back[q, 0].astype(F32)
        sq = back[q, 1, :, 0:1].astype(F32) + back[q, 1, :, HEAD // 2 : HEAD // 2 + 1].astype(F32)
        prefix = term if prefix is None else prefix + term
        square = sq if square is None else square + sq
    prefix = (prefix * lax.rsqrt(square * (1.0 / (CHUNKS * WIDE)) + EPSILON)).astype(BF)
    homes = []
    for k, mate in enumerate(mates):
        outgo[mate[0], 0:CAP] = dot(pack[mate[0]], prefix).astype(BF)
        homes.append(wire.send(outgo.at[mate[0], pl.ds(0, CAP)], outgo.at[g, pl.ds(CAP, CAP)], mate))
    outgo[g, CAP : 2 * CAP] = dot(pack[g], prefix).astype(BF)
    for copy in homes:
        copy.wait_recv()
    result = jnp.zeros((LANES, HEAD), F32)
    for e in range(GROUPS):
        result = result + lax.dot_general(
            unpack[e], outgo[e, CAP : 2 * CAP], (((0,), (0,)), ((), ())), preferred_element_type=F32
        )
    out_ref[...] = result[0:OWN].astype(BF)
    for copy in wire.sent:
        copy.wait_send()


def shards(
    block_tokens, slot_of_row, cache_lengths, embed_table, norm_gain, query_weight, key_value_weight,
    kv_cache, out_weight, final_gain, prefix_weight,
):
    vmem = pl.BlockSpec(memory_space=pltpu.VMEM)
    hbm = pl.BlockSpec(memory_space=pl.ANY)
    return pl.pallas_call(
        kernel,
        out_shape=jax.ShapeDtypeStruct((OWN, HEAD), BF),
        in_specs=[vmem] * 5 + [hbm] * 6,
        out_specs=vmem,
        scratch_shapes=[
            pltpu.VMEM((GROUPS, 16, LANES), jnp.int32),
            pltpu.VMEM((2, VOCAB_ROWS, 2048), BF),
            pltpu.VMEM((CHUNKS * WIDE, 3 * HEAD), BF),
            pltpu.VMEM((QUAD * HEAD, SPAN), BF),
            pltpu.VMEM((SPAN, QUAD * HEAD), BF),
            pltpu.VMEM((GROUPS, OWN, LANES), BF),
            pltpu.VMEM((GROUPS, CAP, OWN), BF),
            pltpu.VMEM((GROUPS, CAP, LANES), BF),
            pltpu.VMEM((2, 2, OWN, VOCAB_ROWS), BF),
            pltpu.VMEM((2, OWN, CACHE, HEAD), BF),
            pltpu.VMEM((2, CACHE, OWN, HEAD), BF),
            pltpu.VMEM((MINE, OWN, WIDE), BF),
            pltpu.VMEM((RING, OWN, WIDE), BF),
            pltpu.VMEM((RING, HALF, WIDE), BF),
            pltpu.VMEM((3, 2, 4, HALF, WIDE), BF),
            pltpu.VMEM((QUAD, 2, 4, QUART, WIDE), BF),
            pltpu.VMEM((HALF, WIDE), BF),
            pltpu.VMEM((CHUNKS, OWN, WIDE), BF),
            pltpu.VMEM((RING, OWN, WIDE), BF),
            pltpu.VMEM((QUAD, OWN, HEAD), BF),
            pltpu.VMEM((OWN, 3 * HEAD), F32),
            pltpu.VMEM((OWN, QUAD * HEAD), F32),
            pltpu.VMEM((OWN, WIDE), F32),
            pltpu.VMEM((QUAD, 2, OWN, HEAD), BF),
            pltpu.VMEM((GROUPS, 2 * CAP, HEAD), BF),
            pltpu.VMEM((QUAD, 2, OWN, HEAD), BF),
            pltpu.SemaphoreType.DMA((7,)),
            pltpu.SemaphoreType.DMA((SEMS,)),
            pltpu.SemaphoreType.DMA((SEMS,)),
        ],
        compiler_params=pltpu.CompilerParams(
            collective_id=0, has_side_effects=True, vmem_limit_bytes=56 * 1024 * 1024
        ),
    )(
        block_tokens.T,
        slot_of_row,
        cache_lengths,
        norm_gain.reshape(2 * CHUNKS, HEAD),
        final_gain.reshape(2 * CHUNKS, HEAD),
        kv_cache,
        embed_table,
        query_weight,
        key_value_weight,
        out_weight,
        prefix_weight,
    )


def solution(mesh):
    in_specs = (
        P("grp", None),
        P("grp"),
        P("grp"),
        P("tp", None),
        P(),
        P(None, "tp"),
        P(None, None, "tp"),
        P(None, "grp", None, "tp"),
        P("tp", None),
        P(),
        P(None, "tp"),
    )
    return jax.shard_map(
        shards, mesh=mesh, in_specs=in_specs, out_specs=P("grp", "tp"), check_vma=False
    )
```

time: 163 us -> 131 us (0.80)
  Pallas kernels: 153 us -> 129 us
  local copies, waits for them, and re-layouts: 9.03 us -> 1.53 us
    pallas_call x1, Pallas kernels: 153 us -> 129 us  [shards(): pl.pallas_call(kernel, out_shape=jax.ShapeDtypeStruct((OWN, HEAD), BF), i...]
    reshape x2 -> x0, local copies, waits for them, and re-layouts: 2.75 us -> none  [the longest x1 1.38 us: shards(): norm_gain.reshape(CHUNKS, WIDE)]
    broadcast_in_dim x2 -> x0, local copies, waits for them, and re-layouts: 2.12 us -> none  [the longest x1 1.44 us: shards(): cache_lengths[:, None]]
    unnamed x2 -> x1, local copies, waits for them, and re-layouts: 3.55 us -> 1.53 us
where the time goes in v2:
time: 131 us; the launch traced here: 130 us
  Pallas kernels  129 us (98%)
  local copies, waits for them, and re-layouts  1.53 us (1%)
    pallas_call x1, Pallas kernels, shards(): pl.pallas_call(kernel, out_shape=jax.ShapeDtypeStruct((OWN, HEAD), BF), i...  129 us

profile of v2, /device:TPU:1, one launch (start us, length us, event | category | flops | bytes accessed | tf_op | source)
XLA Modules:
  0.0 130.4 jit_solution(3449000638399743844)
XLA Ops:
  0.0 128.8 %shard_map.109 = bf16[320,128]{1,0:T(8,128)(2,1)} custom-call(s32[4,320]{1,0:T(4,128)} %bitcast.5, s32[320]{0:T(512)} %slots_ref.1, s32[320]{0:T(512)} %lens_ref.1, f32[64,128]{1,0:T(8,128)} %bitcast.3, f32[64,128]{1,0:T(8,128)} %bitcast.4, bf16[2,320,4,128]{3,2,1,0:T(4,128)(2,1)} %cache_ref.1, bf16[500,2048]{1,0:T(8,128)(2,1)} %table_ref.1, ...), custom_call_target="tpu_custom_call" | custom-call | tf_op jit(solution)/shard_map/pallas_call | solution.py:575
  128.8 1.5 %copy.13 = bf16[320,128]{1,0:T(8,128)(2,1)} copy(bf16[320,128]{1,0:T(8,128)(2,1)} %shard_map.109) | data formatting | bytes 163840

commit v3 on v2

v3 whole, which is shorter than its diff:
```python
import functools

import jax
import jax.numpy as jnp
from jax import lax
from jax.experimental import pallas as pl
from jax.experimental.pallas import tpu as pltpu
from jax.sharding import PartitionSpec as P

MESH = pl.DeviceIdType.MESH
BF = jnp.bfloat16
F32 = jnp.float32
EPSILON = 1e-05
HEAD = 128
CACHE = 4
GROUPS = 8
RING = 8
OWN = 320
HALF = 160
QUART = 80
CAP = 80
LANES = 384
WIDE = 256
CHUNKS = 32
MINE = 16
CORE_SPAN = 1024
VOCAB_ROWS = 500
SEMS = 160
PACK = 80
SLAB = 2 * PACK
NEAR = 7 * SLAB
REST = SLAB
ALL = 8 * SLAB
QKV = 3 * HEAD
PLACES = (0, 2, 4, 6, 7, 5, 3, 1)
FLAG = 16
QUAD = 4
SPAN = 2048


def dot(a, b):
    return jnp.dot(a, b, preferred_element_type=F32)


def dot_lanes(a, b):
    return lax.dot_general(a, b, (((1,), (1,)), ((), ())), preferred_element_type=F32)


def ring_order(i):
    step = (i + 1) // 2
    return 4 + step * (1 - 2 * (i % 2))


class Wire:
    def __init__(self, send_sem, recv_sem):
        self.send_sem, self.recv_sem = send_sem, recv_sem
        self.used = 0
        self.sent = []

    def block(self, count):
        first = self.used
        self.used += count
        assert self.used <= SEMS
        return first

    def make(self, src, dst, peer, index):
        return pltpu.make_async_remote_copy(
            src_ref=src,
            dst_ref=dst,
            send_sem=self.send_sem.at[index],
            recv_sem=self.recv_sem.at[index],
            device_id=peer,
            device_id_type=MESH,
        )

    def send(self, src, dst, peer):
        copy = self.make(src, dst, peer, self.block(1))
        copy.start()
        self.sent.append(copy)
        return copy


class Ring:
    def __init__(self, wire, here, part, land, streams):
        self.wire, self.here, self.part, self.land, self.streams = wire, here, part, land, streams
        self.got = [[[None] * 4, [None] * 4] for _ in streams]

    def zat(self, d):
        return lax.rem(self.here.z + (d + RING), RING)

    def push(self, s, way, k, f, lo, a, n):
        self.got[s][way][k] = self.wire.send(
            self.part.at[f, pl.ds(lo + a, n)],
            self.land.at[s, way, k, pl.ds(a, n)],
            self.here.zp if way == 0 else self.here.zm,
        )

    def hop0(self, s):
        index, lo, n, far, extra = self.streams[s]
        f = index(self.zat(4))
        if extra is not None:
            rows = slice(lo, lo + n)
            self.part[f, rows] = (self.part[f, rows].astype(F32) + extra(0)).astype(BF)
        for way in range(2):
            a, m = far[way]
            if m:
                self.push(s, way, 0, f, lo, a, m)

    def hop(self, k, s):
        index, lo, n, far, extra = self.streams[s]
        part = self.part
        for way in range(2):
            f = index(self.zat(4 - k if way == 0 else k - 4))
            a, m = far[way] if k == 1 else (0, n)
            if self.got[s][way][k - 1] is not None:
                self.got[s][way][k - 1].wait_recv()
            other = None if extra is None else extra(2 * k - 1 + way)
            cuts = sorted({0, a, a + m, n}) if m else [0, n]
            for lo2, hi2 in zip(cuts[:-1], cuts[1:]):
                landed = m > 0 and lo2 >= a and hi2 <= a + m
                if not landed and other is None:
                    continue
                rows = slice(lo + lo2, lo + hi2)
                value = part[f, rows].astype(F32)
                if other is not None:
                    value = value + other[lo2:hi2]
                if landed:
                    value = value + self.land[s, way, k - 1, lo2:hi2].astype(F32)
                part[f, rows] = value.astype(BF)
            self.push(s, way, k, f, lo, 0, n)

    def total(self, s):
        index, lo, n, far, extra = self.streams[s]
        self.got[s][0][3].wait_recv()
        self.got[s][1][3].wait_recv()
        value = self.part[index(self.here.z), lo : lo + n].astype(F32)
        value = value + self.land[s, 0, 3, 0:n].astype(F32) + self.land[s, 1, 3, 0:n].astype(F32)
        return value if extra is None else value + extra(7)


class Share:
    def __init__(self, wire, here, view, streams, seen_from):
        self.wire, self.here, self.view, self.streams, self.seen_from = wire, here, view, streams, seen_from
        self.got = [[[], []] for _ in streams]

    def push(self, s, way, d, a=0, n=None):
        peer, shift = (self.here.zp, -self.seen_from) if way == 0 else (self.here.zm, self.seen_from)
        self.got[s][way].append(
            self.wire.send(self.view(s, d, a, n), self.view(s, d + shift, a, n), peer)
        )

    def begin(self, s):
        self.push(s, 0, 0)
        self.push(s, 1, 0)
        if self.streams[s][1] is not None:
            self.streams[s][1](s, 0)

    def hop(self, k, s):
        far, tap = self.streams[s]
        for way in range(2):
            d = -k if way == 0 else k
            if k == 4:
                if far[way][1]:
                    self.got[s][way][3].wait_recv()
                continue
            self.got[s][way][k - 1].wait_recv()
            if k < 3:
                self.push(s, way, d)
            elif far[way][1]:
                self.push(s, way, d, *far[way])
            if tap is not None:
                tap(s, d)
        if k == 4 and tap is not None:
            tap(s, 4)


SPLIT = ((0, 1), (1, 1))
UP = ((0, QUART), (0, 0))
DOWN = ((0, 0), (0, QUART))


def gain_row(gain_ref, i):
    return jnp.concatenate([gain_ref[pl.ds(2 * i, 1), :], gain_ref[pl.ds(2 * i + 1, 1), :]], axis=1)


class Here:
    pass


def kernel(
    tokens_ref, slots_ref, lens_ref, gain_ref, final_ref, cache_ref, table_ref, wq_ref, wkv_ref, wo_ref,
    wp_ref, out_ref, flag_ref,
    info, tabs, wqkv, folded, product, staged, woq, wpq, member, pack, unpack, upto, packed, near_hot, rest_hot, natural, cache, part2,
    land2, full1, full2, att, acc, acc4, squares, partial, sums_in, outgo, back, local_sem,
    send_sem, recv_sem,
):
    g = lax.axis_index("grp")
    t = lax.axis_index("tp")
    here = Here()
    core = here.core = t % 2
    z = here.z = (t // 2) % RING
    xl = here.xl = t // (2 * RING)
    quarter = core * 2 + xl

    def place(x, zz, cc):
        return (x * RING + zz) * 2 + cc

    here.zp = (g, place(xl, lax.rem(z + 1, RING), core))
    here.zm = (g, place(xl, lax.rem(z + RING - 1, RING), core))
    here.xm = (g, place(1 - xl, z, core))
    here.cp = (g, place(xl, z, 1 - core))
    dg = (g, place(1 - xl, z, 1 - core))
    og = lax.rem(g + GROUPS // 2, GROUPS)
    xm_other = (og, here.xm[1])
    dg_other = (og, dg[1])
    cp_quarter = (1 - core) * 2 + xl
    xm_quarter = core * 2 + (1 - xl)
    dg_quarter = (1 - core) * 2 + (1 - xl)
    mates = [(lax.rem(g + k, GROUPS), t) for k in range(1, GROUPS)]

    def wide(i, n):
        return pl.ds(pl.multiple_of(i * n, n), n)

    def table_half(c):
        return table_ref.at[:, pl.ds(pl.multiple_of(c * CORE_SPAN, CORE_SPAN), CORE_SPAN)]

    table_load = pltpu.make_async_copy(table_half(core), tabs.at[core], local_sem.at[0])
    loads = [
        pltpu.make_async_copy(cache_ref, natural, local_sem.at[6]),
        pltpu.make_async_copy(wq_ref, wqkv.at[:, pl.ds(0, HEAD)], local_sem.at[1]),
        pltpu.make_async_copy(wkv_ref.at[0], wqkv.at[:, pl.ds(HEAD, HEAD)], local_sem.at[2]),
        pltpu.make_async_copy(wkv_ref.at[1], wqkv.at[:, pl.ds(2 * HEAD, HEAD)], local_sem.at[3]),
        pltpu.make_async_copy(wo_ref.at[:, wide(quarter, SPAN)], woq.at[quarter], local_sem.at[4]),
        pltpu.make_async_copy(wp_ref.at[wide(quarter, SPAN)], wpq.at[quarter], local_sem.at[5]),
    ]
    others = [cp_quarter, xm_quarter, dg_quarter]
    stages = [
        pltpu.make_async_copy(wo_ref.at[:, wide(q, SPAN)], staged.at[q], local_sem.at[7 + n])
        for n, q in enumerate(others)
    ]
    table_load.start()
    for stage in stages:
        stage.start()
    info[g] = jnp.full((16, LANES), -1, jnp.int32)
    info[g, 0:4, 0:OWN] = tokens_ref[...]
    info[g, 8:9, 0:OWN] = slots_ref[...].reshape(1, OWN)

    barrier = pltpu.get_barrier_semaphore()
    peers = [here.zp, here.zm, here.xm, here.cp, dg, xm_other, dg_other] + mates
    for peer in peers:
        pl.semaphore_signal(barrier, inc=1, device_id=peer, device_id_type=MESH)
    pl.semaphore_wait(barrier, len(peers))

    wire = Wire(send_sem, recv_sem)
    told = [wire.send(info.at[g], info.at[g], mate) for mate in mates]
    table_in = wire.send(table_half(1 - core), tabs.at[core], here.cp)
    for load in loads:
        load.start()

    for stage in stages:
        stage.wait()
    receivers = list(zip((here.cp, xm_other, dg_other), others))
    wo_in = [wire.send(staged.at[q], woq.at[quarter], who) for who, q in receivers]
    upto[...] = (
        lax.broadcasted_iota(jnp.int32, (512, 512), 0) <= lax.broadcasted_iota(jnp.int32, (512, 512), 1)
    ).astype(F32).astype(BF)
    for copy in told:
        copy.wait_recv()

    slots = lax.broadcasted_iota(jnp.int32, (OWN, LANES), 0) + g * OWN
    down = jnp.zeros((OWN, 8), F32)
    across = jnp.zeros((8, OWN), F32)
    for e in range(GROUPS):
        hit = (info[e, 8:9, :] == slots).astype(F32).astype(BF)
        member[e] = hit
        heard = info[e, 0:4, :]
        heard = jnp.concatenate([heard >> 7, heard & 127], axis=0).astype(F32).astype(BF)
        down = down + dot_lanes(hit, heard)
        across = across + dot_lanes(heard, hit)
    ids = down[:, 0:4] * 128.0 + down[:, 4:8]
    ids_across = across[0:4] * 128.0 + across[4:8]

    local = (ids - ((xl * RING + z) * (2 * VOCAB_ROWS)).astype(F32)).astype(jnp.int32)
    names = lax.broadcasted_iota(jnp.int32, (OWN, 512), 1)
    seen = []
    for e in range(2):
        hits = jnp.zeros((OWN, 512), F32)
        for j in range(4):
            hits = jnp.where(local[:, j : j + 1] - e * VOCAB_ROWS == names, 1.0, hits)
        seen.append(jnp.where(names[0:1] < VOCAB_ROWS, jnp.max(hits, axis=0, keepdims=True), 0.0))
    ranks = dot(jnp.concatenate(seen, axis=0).astype(BF), upto[...])
    ranks = [ranks[0:1], ranks[1:2] + ranks[0:1, 511:512]]
    order = lax.broadcasted_iota(jnp.int32, (PACK, 512), 0).astype(F32) + 1.0
    picks = [jnp.where(ranks[e] == order, seen[e], 0.0).astype(BF)[:, 0:VOCAB_ROWS] for e in range(2)]

    table_load.wait()
    table_in.wait_recv()
    for e in range(4):
        columns = slice(e * WIDE, (e + 1) * WIDE)
        value = dot(picks[0], tabs[0, :, columns]) + dot(picks[1], tabs[1, :, columns])
        packed[core * 4 + e, 0, xl] = value.astype(BF)

    gxx, gc = {}, {}

    def view(s, d, first=0, n=None):
        side = 1 - xl if s == 2 else xl
        at = core * 4 + (0 if s == 0 else 2) + first
        return packed.at[pl.ds(at, 2 if n is None else n), PLACES[d % RING], side]

    def beyond(s, d):
        ref = view(s, d)
        gxx[d] = wire.send(ref, ref, here.xm)
        gc[s, d] = wire.send(ref, ref, here.cp)

    def beside(s, d):
        ref = view(s, d)
        gc[s, d] = wire.send(ref, ref, here.cp)

    def late(d):
        gxx[d].wait_recv()
        ref = packed.at[pl.ds(core * 4, 2), PLACES[d % RING], 1 - xl]
        gc[3, d] = wire.send(ref, ref, here.cp)

    share = Share(wire, here, view, [(SPLIT, beyond), (SPLIT, beside), (SPLIT, beside)], 1)
    ref = view(1, 0)
    swap = wire.send(ref, ref, here.xm)
    share.begin(0)
    share.begin(1)
    for load in loads:
        load.wait()
    for k in range(2):
        for b in range(4):
            rows = slice(b * 80, b * 80 + 80)
            block = natural[k, rows].astype(F32)
            for c in range(CACHE):
                cache[k, c, rows] = block[:, c, :].astype(BF)
    swap.wait_recv()
    share.begin(2)
    for s in range(3):
        share.hop(1, s)
    late(0)

    shares = jnp.floor((ids + 0.5) * (0.5 / VOCAB_ROWS))
    lowest = shares * (2.0 * VOCAB_ROWS)
    earlier = lax.broadcasted_iota(jnp.int32, (OWN, OWN), 0) < lax.broadcasted_iota(
        jnp.int32, (OWN, OWN), 1
    )
    firsts = []
    for j in range(4):
        row = ids_across[j : j + 1]
        again = jnp.where(earlier & (ids[:, j : j + 1] == row), 1.0, 0.0)
        for i in range(j):
            again = jnp.where(ids[:, i : i + 1] == row, 1.0, again)
        firsts.append(jnp.where(jnp.max(again, axis=0, keepdims=True) > 0.0, -1.0, row))
    rank = []
    for j in range(4):
        below = jnp.zeros((OWN, OWN), F32)
        for i in range(4):
            inside = (firsts[i] >= lowest[:, j : j + 1]) & (firsts[i] < ids[:, j : j + 1])
            below = below + jnp.where(inside, 1.0, 0.0)
        rank.append(jnp.sum(below, axis=1, keepdims=True))
    rank = jnp.concatenate(rank, axis=1)
    over = jnp.max(jnp.where(rank >= PACK, 1.0, 0.0))
    column = jnp.where(shares >= RING, 1.0, 0.0)
    apart = shares - column * RING - z.astype(F32)
    apart = jnp.where(apart < 0.0, apart + RING, apart)
    slab = jnp.where(apart < 4.0, 2.0 * apart, jnp.where(apart == 4.0, 7.0, 15.0 - 2.0 * apart))
    spot = (slab * SLAB + column * PACK + rank).astype(jnp.int32)
    for j in range(4):
        near_hot[j] = (
            spot[:, j : j + 1] == lax.broadcasted_iota(jnp.int32, (OWN, NEAR), 1)
        ).astype(F32).astype(BF)
        rest_hot[j] = (
            spot[:, j : j + 1] - NEAR == lax.broadcasted_iota(jnp.int32, (OWN, REST), 1)
        ).astype(F32).astype(BF)

    for s in range(3):
        share.hop(2, s)
    late(-1)
    late(1)

    corner = lax.broadcasted_iota(jnp.int32, (WIDE, WIDE), 0) == lax.broadcasted_iota(
        jnp.int32, (WIDE, WIDE), 1
    )

    def fold(f, carry):
        for j in range(4):
            i = j * 8 + f
            gain = jnp.sum(jnp.where(corner, gain_row(gain_ref, i), 0.0), axis=1, keepdims=True)
            folded[wide(f, WIDE), j * QKV : (j + 1) * QKV] = (
                wqkv[wide(i, WIDE), :].astype(F32) * gain
            ).astype(BF)
        return carry

    lax.fori_loop(0, 8, fold, 0)

    def arrived(*apart):
        for s in range(4):
            for d in apart:
                gc[s, d].wait_recv()

    def multiply(a, b):
        rows = slice(a * SLAB, b * SLAB)
        count = (b - a) * SLAB

        def step(n, carry):
            left = [packed[f, a:b].reshape(count, WIDE) for f in range(8)]
            value = dot(jnp.concatenate(left, axis=1), folded[:, wide(n, WIDE)])
            product[rows, wide(n, WIDE)] = value.astype(BF)
            return carry

        lax.fori_loop(0, 4 * QKV // WIDE, step, 0)
        sq = None
        for f in range(8):
            value = packed[f, a:b].reshape(count, WIDE).astype(F32)
            sq = value * value if sq is None else sq + value * value
        sq = jnp.sum(sq, axis=1, keepdims=True)
        high = sq.astype(BF).astype(F32)
        lanes = lax.broadcasted_iota(jnp.int32, (count, HEAD), 1)
        product[rows, 4 * QKV :] = jnp.where(lanes < HEAD // 2, high, sq - high).astype(BF)

    def pick(hot, rows):
        total = None
        for j in range(4):
            right = [product[rows, j * QKV : (j + 1) * QKV], product[rows, 4 * QKV :]]
            term = dot(hot[j], jnp.concatenate(right, axis=1))
            total = term if total is None else total + term
        return total

    for s in range(3):
        share.hop(3, s)
    late(-2)
    late(2)
    wp_in = [wire.send(wp_ref.at[wide(q, SPAN)], wpq.at[quarter], who) for who, q in receivers]
    arrived(0, -1, 1)
    multiply(0, 3)
    for s in range(3):
        share.hop(4, s)
    late(-3)
    late(3)
    arrived(-2, 2)
    multiply(3, 5)
    late(4)
    arrived(-3, 3)
    multiply(5, 7)
    acc[...] = pick(near_hot, slice(0, NEAR))
    arrived(4)
    multiply(7, 8)
    acc[...] += pick(rest_hot, slice(NEAR, ALL))
    square = acc[:, QKV : QKV + 1] + acc[:, QKV + HEAD // 2 : QKV + HEAD // 2 + 1]
    scale = lax.rsqrt(square * (1.0 / (CHUNKS * WIDE)) + EPSILON)

    queries = (acc[:, 0:HEAD] * scale).astype(BF).astype(F32)
    keys = (acc[:, HEAD : 2 * HEAD] * scale).astype(BF).astype(F32)
    values = (acc[:, 2 * HEAD : QKV] * scale).astype(BF).astype(F32)
    root = 1.0 / HEAD**0.5
    diagonal = lax.broadcasted_iota(jnp.int32, (OWN, OWN), 0) == lax.broadcasted_iota(
        jnp.int32, (OWN, OWN), 1
    )
    lens = jnp.sum(
        jnp.where(diagonal, lens_ref[...].reshape(1, OWN).astype(F32), 0.0), axis=1, keepdims=True
    )
    scores = []
    for c in range(CACHE):
        s = jnp.sum(queries * cache[0, c].astype(F32), axis=1, keepdims=True) * root
        scores.append(jnp.where(lens > c + 0.5, s, -1e30))
    scores.append(jnp.sum(queries * keys, axis=1, keepdims=True) * root)
    top = functools.reduce(jnp.maximum, scores)
    raised = [jnp.exp(s - top) for s in scores]
    whole = functools.reduce(jnp.add, raised)
    weights = [(r / whole).astype(BF).astype(F32) for r in raised]
    mixed = weights[CACHE] * values
    for c in range(CACHE):
        mixed = mixed + weights[c] * cache[1, c].astype(F32)
    att[quarter] = mixed.astype(BF)
    att_in = [wire.send(att.at[quarter], att.at[quarter], who) for who in (here.xm, dg, here.cp)]

    upper = (
        lax.broadcasted_iota(jnp.int32, (LANES, LANES), 0)
        <= lax.broadcasted_iota(jnp.int32, (LANES, LANES), 1)
    ).astype(F32).astype(BF)
    places = lax.broadcasted_iota(jnp.int32, (CAP, LANES), 0).astype(F32)
    own_slots = info[g, 8:9, :]
    for e in range(GROUPS):
        row = info[e, 8:9, :] - g * OWN
        inside = ((row >= 0) & (row < OWN)).astype(F32)
        rank = dot(inside.astype(BF), upper)
        pick = jnp.where(rank - 1.0 == places, inside, 0.0).astype(BF)
        pack[e] = dot_lanes(pick, member[e]).astype(BF)
        row = own_slots - e * OWN
        inside = ((row >= 0) & (row < OWN)).astype(F32)
        rank = dot(inside.astype(BF), upper)
        unpack[e] = jnp.where(rank - 1.0 == places, inside, 0.0).astype(BF)

    def lay(f, carry):
        full1[f] = (
            dot(near_hot[quarter], packed[f, 0:7].reshape(NEAR, WIDE))
            + dot(rest_hot[quarter], packed[f, 7].reshape(REST, WIDE))
        ).astype(BF)
        return carry

    lax.fori_loop(0, 8, lay, 0)
    for copy in att_in + wo_in:
        copy.wait_recv()

    def spread(i, carry):
        zz = lax.rem(z + ring_order(i), RING)
        both = jnp.concatenate([att[q] for q in range(QUAD)], axis=1)
        blocks = [woq[q, :, wide(zz, WIDE)] for q in range(QUAD)]
        part2[zz] = dot(both, jnp.concatenate(blocks, axis=0)).astype(BF)
        return carry

    strips = [(lambda zz: zz, QUART * s, QUART, (UP, DOWN)[s % 2], None) for s in range(QUAD)]
    ring = Ring(wire, here, part2, land2, strips)
    spread(0, 0)
    for s in range(QUAD):
        ring.hop0(s)
    lax.fori_loop(1, RING, spread, 0)
    for k in (1, 2, 3):
        for s in range(QUAD):
            ring.hop(k, s)

    def strip(s, d, first=0, n=QUART):
        return full2.at[ring.zat(d), pl.ds(QUART * s + first, n)]

    share = Share(
        wire, here, lambda s, d, a, n: strip(s, d, 0, QUART), [(far, None) for _, _, _, far, _ in strips], 0
    )
    for s in range(QUAD):
        rows = slice(QUART * s, QUART * s + QUART)
        value = ring.total(s) + full1[z, rows].astype(F32)
        full2[z, rows] = value.astype(BF)
        share.begin(s)

    def take(zz, first):
        value = full2[zz].astype(F32)
        scaled = (value * gain_row(final_ref, quarter * RING + zz)).astype(BF)
        blocks = [wpq[q, wide(zz, WIDE), :] for q in range(QUAD)]
        term = dot(scaled, jnp.concatenate(blocks, axis=1))
        if first:
            acc4[...] = term
            squares[...] = value * value
        else:
            acc4[...] += term
            squares[...] += value * value

    for copy in wp_in:
        copy.wait_recv()
    take(z, True)
    for k in (1, 2, 3, 4):
        for s in range(QUAD):
            share.hop(k, s)
        take(ring.zat(-k), False)
        if k < 4:
            take(ring.zat(k), False)

    for q in range(QUAD):
        partial[q] = acc4[:, q * HEAD : (q + 1) * HEAD].astype(BF)
    mine = [
        wire.send(partial.at[q], back.at[quarter], who)
        for who, q in ((here.xm, xm_quarter), (dg, dg_quarter), (here.cp, cp_quarter))
    ]
    square = lax.dot_general(
        jnp.ones((8, WIDE), F32),
        squares[...],
        (((1,), (1,)), ((), ())),
        preferred_element_type=F32,
        precision=lax.Precision.HIGHEST,
    )
    sums_in[quarter] = square
    mine += [
        wire.send(sums_in.at[quarter], sums_in.at[quarter], who) for who in (here.xm, dg, here.cp)
    ]
    back[quarter] = partial[quarter]
    for copy in mine:
        copy.wait_recv()
    prefix, square = None, None
    for q in range(QUAD):
        term = back[q].astype(F32)
        prefix = term if prefix is None else prefix + term
        square = sums_in[q, 0:1] if square is None else square + sums_in[q, 0:1]
    square = lax.rsqrt(square * (1.0 / (CHUNKS * WIDE)) + EPSILON)
    square = jnp.sum(jnp.where(diagonal, square, 0.0), axis=1, keepdims=True)
    prefix = (prefix * square).astype(BF)
    homes = []
    away = CAP + FLAG
    for e in range(GROUPS):
        outgo[e, CAP:away] = jnp.full((FLAG, HEAD), over, F32).astype(BF)
    for k, mate in enumerate(mates):
        outgo[mate[0], 0:CAP] = dot(pack[mate[0]], prefix).astype(BF)
        homes.append(wire.send(outgo.at[mate[0], pl.ds(0, away)], outgo.at[g, pl.ds(away, away)], mate))
    outgo[g, away : away + CAP] = dot(pack[g], prefix).astype(BF)
    outgo[g, away + CAP : 2 * away] = jnp.full((FLAG, HEAD), over, F32).astype(BF)
    for copy in homes:
        copy.wait_recv()
    result = jnp.zeros((LANES, HEAD), F32)
    flag = jnp.zeros((FLAG, HEAD), F32)
    for e in range(GROUPS):
        flag = jnp.maximum(flag, outgo[e, away + CAP : 2 * away].astype(F32))
        result = result + lax.dot_general(
            unpack[e], outgo[e, away : away + CAP], (((0,), (0,)), ((), ())), preferred_element_type=F32
        )
    out_ref[...] = result[0:OWN].astype(BF)
    flag_ref[...] = flag[0:8].astype(jnp.int32)
    for copy in wire.sent:
        copy.wait_send()


def sum_shares(rows):
    count = lax.axis_size("tp")
    blocks = rows.reshape(rows.shape[0], count, -1).transpose(1, 0, 2)
    blocks = lax.all_to_all(blocks, "tp", split_axis=0, concat_axis=0, tiled=True)
    return jnp.sum(blocks.astype(jnp.float32), axis=0)


def all_shares(rows):
    count = lax.axis_size("tp")
    blocks = jnp.broadcast_to(rows[None], (count,) + rows.shape)
    blocks = lax.all_to_all(blocks, "tp", split_axis=0, concat_axis=0, tiled=True)
    return blocks.transpose(1, 0, 2).reshape(rows.shape[0], -1)


def rms_scale(rows, gain):
    values = rows.astype(jnp.float32)
    spread = jnp.mean(values * values, axis=-1, keepdims=True)
    return (values * lax.rsqrt(spread + EPSILON) * gain).astype(jnp.bfloat16)


def routing(slot_ids, owned, groups, capacity):
    target = slot_ids // owned
    place_in = slot_ids % owned
    member = (target[:, None] == jnp.arange(groups, dtype=jnp.int32)[None, :]).astype(jnp.int32)
    within = jnp.sum((jnp.cumsum(member, axis=0) - 1) * member, axis=1)
    return (target * capacity + within, place_in)


def pack_rows(values, slot_index, total):
    buffer = jnp.zeros((total,) + values.shape[1:], values.dtype)
    return buffer.at[slot_index].set(values)


def lookup_part(token_ids, table):
    vocab_rows = table.shape[0]
    local_ids = token_ids - lax.axis_index("tp") * vocab_rows
    inside = (local_ids >= 0) & (local_ids < vocab_rows)
    picked = jnp.take(table, jnp.clip(local_ids, 0, vocab_rows - 1), axis=0)
    picked = jnp.where(inside[..., None], picked, jnp.zeros_like(picked))
    return picked.reshape(token_ids.shape[0], -1).astype(jnp.float32)


def attend(normed, query_weight, key_value_weight, kv_cache, cache_lengths):
    row_count = normed.shape[0]
    queries = jnp.dot(normed, query_weight, preferred_element_type=jnp.float32).astype(jnp.bfloat16)
    fresh = jnp.einsum(
        "rg,kgd->krd", normed, key_value_weight, preferred_element_type=jnp.float32
    ).astype(jnp.bfloat16)
    heads_here = queries.shape[1] // HEAD
    query_heads = queries.reshape(row_count, heads_here, HEAD)
    key_heads = fresh[0].reshape(row_count, heads_here, HEAD)
    value_heads = fresh[1].reshape(row_count, heads_here, HEAD)
    cached = kv_cache.reshape(2, row_count, CACHE, heads_here, HEAD)
    scale = 1.0 / HEAD**0.5
    past = (
        jnp.einsum("rhd,rchd->rhc", query_heads, cached[0], preferred_element_type=jnp.float32)
        * scale
    )
    valid = jnp.arange(CACHE, dtype=jnp.int32)[None, None, :] < cache_lengths[:, None, None]
    past = jnp.where(valid, past, jnp.float32(-1e30))
    own_score = (
        jnp.sum(query_heads.astype(jnp.float32) * key_heads.astype(jnp.float32), axis=-1)[..., None]
        * scale
    )
    weights = jax.nn.softmax(jnp.concatenate([past, own_score], axis=-1), axis=-1).astype(
        jnp.bfloat16
    )
    mixed = jnp.einsum(
        "rhc,rchd->rhd", weights[..., :-1], cached[1], preferred_element_type=jnp.float32
    )
    mixed = mixed + weights[..., -1:].astype(jnp.float32) * value_heads.astype(jnp.float32)
    return mixed.reshape(row_count, -1).astype(jnp.bfloat16)


def plain(
    block_tokens,
    slot_of_row,
    cache_lengths,
    embed_table,
    norm_gain,
    query_weight,
    key_value_weight,
    kv_cache,
    out_weight,
    final_gain,
    prefix_weight,
):
    groups = lax.axis_size("grp")
    owned = slot_of_row.shape[0]
    capacity = 2 * owned // groups
    total = groups * capacity
    slot_index, place_in = routing(slot_of_row, owned, groups, capacity)
    sent_place = (
        jnp.full((total,), owned, jnp.int32).at[slot_index].set(place_in).reshape(groups, capacity)
    )
    shares = sum_shares(lookup_part(block_tokens, embed_table).astype(jnp.bfloat16)).astype(jnp.bfloat16)
    sent_rows = pack_rows(shares, slot_index, total).reshape(groups, capacity, -1)
    got_rows, got_place = (
        lax.all_to_all(sent_rows, "grp", split_axis=0, concat_axis=0, tiled=True),
        lax.all_to_all(sent_place, "grp", split_axis=0, concat_axis=0, tiled=True),
    )
    got_place = got_place.reshape(total)
    own_part = (
        jnp.zeros((owned, shares.shape[1]), jnp.bfloat16)
        .at[got_place]
        .set(got_rows.reshape(total, -1), mode="drop")
    )
    whole = all_shares(own_part)
    normed = rms_scale(whole, norm_gain)
    attended = attend(normed, query_weight, key_value_weight, kv_cache, cache_lengths)
    partial_value = jnp.dot(attended, out_weight, preferred_element_type=jnp.float32)
    summed = sum_shares(partial_value.astype(jnp.bfloat16))
    context = (own_part.astype(jnp.float32) + summed).astype(jnp.bfloat16)
    source_rows = jnp.minimum(got_place, owned - 1)
    back_rows = jnp.take(context, source_rows, axis=0).reshape(groups, capacity, -1)
    home_rows = lax.all_to_all(back_rows, "grp", split_axis=0, concat_axis=0, tiled=True).reshape(
        total, -1
    )
    mine = jnp.take(home_rows, slot_index, axis=0)
    full_rows = all_shares(mine)
    return jnp.dot(
        rms_scale(full_rows, final_gain), prefix_weight, preferred_element_type=jnp.float32
    ).astype(jnp.bfloat16)


def shards(
    block_tokens, slot_of_row, cache_lengths, embed_table, norm_gain, query_weight, key_value_weight,
    kv_cache, out_weight, final_gain, prefix_weight,
):
    vmem = pl.BlockSpec(memory_space=pltpu.VMEM)
    hbm = pl.BlockSpec(memory_space=pl.ANY)
    out, flag = pl.pallas_call(
        kernel,
        out_shape=[jax.ShapeDtypeStruct((OWN, HEAD), BF), jax.ShapeDtypeStruct((8, HEAD), jnp.int32)],
        in_specs=[vmem] * 5 + [hbm] * 6,
        out_specs=[vmem, vmem],
        scratch_shapes=[
            pltpu.VMEM((GROUPS, 16, LANES), jnp.int32),
            pltpu.VMEM((2, VOCAB_ROWS, CORE_SPAN), BF),
            pltpu.VMEM((CHUNKS * WIDE, 3 * HEAD), BF),
            pltpu.VMEM((SPAN, 4 * QKV), BF),
            pltpu.VMEM((ALL, 4 * QKV + HEAD), BF),
            pltpu.VMEM((QUAD, HEAD, SPAN), BF),
            pltpu.VMEM((QUAD, HEAD, SPAN), BF),
            pltpu.VMEM((QUAD, SPAN, HEAD), BF),
            pltpu.VMEM((GROUPS, OWN, LANES), BF),
            pltpu.VMEM((GROUPS, CAP, OWN), BF),
            pltpu.VMEM((GROUPS, CAP, LANES), BF),
            pltpu.VMEM((512, 512), BF),
            pltpu.VMEM((8, RING, 2, PACK, WIDE), BF),
            pltpu.VMEM((4, OWN, NEAR), BF),
            pltpu.VMEM((4, OWN, REST), BF),
            pltpu.VMEM((2, OWN, CACHE, HEAD), BF),
            pltpu.VMEM((2, CACHE, OWN, HEAD), BF),
            pltpu.VMEM((RING, OWN, WIDE), BF),
            pltpu.VMEM((QUAD, 2, 4, QUART, WIDE), BF),
            pltpu.VMEM((RING, OWN, WIDE), BF),
            pltpu.VMEM((RING, OWN, WIDE), BF),
            pltpu.VMEM((QUAD, OWN, HEAD), BF),
            pltpu.VMEM((OWN, QUAD * HEAD), F32),
            pltpu.VMEM((OWN, QUAD * HEAD), F32),
            pltpu.VMEM((OWN, WIDE), F32),
            pltpu.VMEM((QUAD, OWN, HEAD), BF),
            pltpu.VMEM((QUAD, 8, OWN), F32),
            pltpu.VMEM((GROUPS, 2 * (CAP + FLAG), HEAD), BF),
            pltpu.VMEM((QUAD, OWN, HEAD), BF),
            pltpu.SemaphoreType.DMA((10,)),
            pltpu.SemaphoreType.DMA((SEMS,)),
            pltpu.SemaphoreType.DMA((SEMS,)),
        ],
        compiler_params=pltpu.CompilerParams(
            collective_id=0, has_side_effects=True, vmem_limit_bytes=60 * 1024 * 1024
        ),
    )(
        block_tokens.T,
        slot_of_row,
        cache_lengths,
        norm_gain.reshape(2 * CHUNKS, HEAD),
        final_gain.reshape(2 * CHUNKS, HEAD),
        kv_cache,
        embed_table,
        query_weight,
        key_value_weight,
        out_weight,
        prefix_weight,
    )
    return lax.cond(
        flag[0, 0] > 0,
        lambda: plain(
            block_tokens, slot_of_row, cache_lengths, embed_table, norm_gain, query_weight,
            key_value_weight, kv_cache, out_weight, final_gain, prefix_weight,
        ),
        lambda: out,
    )


def solution(mesh):
    in_specs = (
        P("grp", None),
        P("grp"),
        P("grp"),
        P("tp", None),
        P(),
        P(None, "tp"),
        P(None, None, "tp"),
        P(None, "grp", None, "tp"),
        P("tp", None),
        P(),
        P(None, "tp"),
    )
    return jax.shard_map(
        shards, mesh=mesh, in_specs=in_specs, out_specs=P("grp", "tp"), check_vma=False
    )
```

time: 131 us -> 108 us (0.82)
  Pallas kernels: 129 us -> 105 us
    pallas_call x1, Pallas kernels: 129 us -> 105 us  [shards(): pl.pallas_call(kernel, out_shape=[jax.ShapeDtypeStruct((OWN, HEAD), BF),...]
where the time goes in v3:
time: 108 us
  Pallas kernels  105 us (97%)
  local copies, waits for them, and re-layouts  1.86 us (2%)
    pallas_call x1, Pallas kernels, shards(): pl.pallas_call(kernel, out_shape=[jax.ShapeDtypeStruct((OWN, HEAD), BF),...  105 us

profile of v3, /device:TPU:1, one launch (start us, length us, event | category | flops | bytes accessed | tf_op | source)
XLA Modules:
  0.0 108.1 jit_solution(4449824521375563410)
XLA Ops:
  0.0 0.0 copy-start
  0.0 0.0 copy-start.4
  0.0 0.0 copy-start.5
  0.0 0.0 copy-start.6
  0.0 0.0 copy-start.7
  0.0 0.0 copy-start.8
  0.0 0.0 copy-start.9
  0.0 105.2 %shard_map.111 = (bf16[320,128]{1,0:T(8,128)(2,1)S(1)}, s32[8,128]{1,0:T(8,128)}) custom-call(s32[4,320]{1,0:T(4,128)} %bitcast.99, s32[320]{0:T(512)} %slots_ref.1, s32[320]{0:T(512)} %lens_ref.1, f32[64,128]{1,0:T(8,128)} %bitcast.93, f32[64,128]{1,0:T(8,128)} %bitcast.95, bf16[2,320,4,128]{3,2,1,0:T(4,128)(2,1)} %cache_ref.1, ...), custom_call_target="tpu_custom_call" | custom-call | tf_op jit(solution)/shard_map/pallas_call | solution.py:740
  105.2 1.2 %slice.32 = s32[1,1]{1,0:T(1,128)} slice(s32[8,128]{1,0:T(8,128)} %get-tuple-element.44), slice={[0:1], [0:1]} | slice | bytes 8 | tf_op jit(solution)/shard_map/slice | solution.py:796
  107.1 0.0 copy-done
  107.1 0.0 copy-done.4
  107.1 0.0 copy-done.5
  107.1 0.0 copy-done.6
  107.1 0.0 copy-done.7
  107.1 0.0 copy-done.8
  107.2 0.0 copy-done.9
  107.2 0.3 conditional.1
  107.4 0.6 copy.57
Async XLA Ops:
  0.0 107.1 %copy-start = (bf16[500,2048]{1,0:T(8,128)(2,1)S(1)}, bf16[500,2048]{1,0:T(8,128)(2,1)}, u32[]{:S(2)}) copy-start(bf16[500,2048]{1,0:T(8,128)(2,1)} %table_ref.1) | copy-start | bytes 6144004
  0.0 107.1 %copy-start.4 = (f32[8192]{0:T(1024)S(1)}, f32[8192]{0:T(1024)}, u32[]{:S(2)}) copy-start(f32[8192]{0:T(1024)} %param.17) | copy-start | bytes 98308
  0.0 107.1 %copy-start.5 = (bf16[2,320,4,128]{3,2,1,0:T(4,128)(2,1)S(1)}, bf16[2,320,4,128]{3,2,1,0:T(4,128)(2,1)}, u32[]{:S(2)}) copy-start(bf16[2,320,4,128]{3,2,1,0:T(4,128)(2,1)} %cache_ref.1) | copy-start | bytes 1966084
  0.0 107.1 %copy-start.6 = (f32[8192]{0:T(1024)S(1)}, f32[8192]{0:T(1024)}, u32[]{:S(2)}) copy-start(f32[8192]{0:T(1024)} %param.22) | copy-start | bytes 98308
  0.0 107.1 %copy-start.7 = (s32[320,4]{0,1:T(4,128)S(1)}, s32[320,4]{0,1:T(4,128)}, u32[]{:S(2)}) copy-start(s32[320,4]{0,1:T(4,128)} %param.13) | copy-start | bytes 15364
  0.0 107.1 %copy-start.8 = (s32[320]{0:T(512)S(1)}, s32[320]{0:T(512)}, u32[]{:S(2)}) copy-start(s32[320]{0:T(512)} %slots_ref.1) | copy-start | bytes 3844
  0.0 107.1 %copy-start.9 = (s32[320]{0:T(512)S(1)}, s32[320]{0:T(512)}, u32[]{:S(2)}) copy-start(s32[320]{0:T(512)} %lens_ref.1) | copy-start | bytes 3844

commit v4 on v3

--- a/solution.py
+++ b/solution.py
@@ -239,8 +239,8 @@
         for n, q in enumerate(others)
     ]
     table_load.start()
-    for stage in stages:
-        stage.start()
+    for copy in stages + loads:
+        copy.start()
     info[g] = jnp.full((16, LANES), -1, jnp.int32)
     info[g, 0:4, 0:OWN] = tokens_ref[...]
     info[g, 8:9, 0:OWN] = slots_ref[...].reshape(1, OWN)
@@ -254,8 +254,6 @@
     wire = Wire(send_sem, recv_sem)
     told = [wire.send(info.at[g], info.at[g], mate) for mate in mates]
     table_in = wire.send(table_half(1 - core), tabs.at[core], here.cp)
-    for load in loads:
-        load.start()
 
     for stage in stages:
         stage.wait()
@@ -264,6 +262,29 @@
     upto[...] = (
         lax.broadcasted_iota(jnp.int32, (512, 512), 0) <= lax.broadcasted_iota(jnp.int32, (512, 512), 1)
     ).astype(F32).astype(BF)
+    for load in loads:
+        load.wait()
+    for k in range(2):
+        for b in range(4):
+            rows = slice(b * 80, b * 80 + 80)
+            block = natural[k, rows].astype(F32)
+            for c in range(CACHE):
+                cache[k, c, rows] = block[:, c, :].astype(BF)
+
+    corner = lax.broadcasted_iota(jnp.int32, (WIDE, WIDE), 0) == lax.broadcasted_iota(
+        jnp.int32, (WIDE, WIDE), 1
+    )
+
+    def fold(f, carry):
+        for j in range(4):
+            i = j * 8 + f
+            gain = jnp.sum(jnp.where(corner, gain_row(gain_ref, i), 0.0), axis=1, keepdims=True)
+            folded[wide(f, WIDE), j * QKV : (j + 1) * QKV] = (
+                wqkv[wide(i, WIDE), :].astype(F32) * gain
+            ).astype(BF)
+        return carry
+
+    lax.fori_loop(0, 8, fold, 0)
     for copy in told:
         copy.wait_recv()
 
@@ -326,14 +347,6 @@
     swap = wire.send(ref, ref, here.xm)
     share.begin(0)
     share.begin(1)
-    for load in loads:
-        load.wait()
-    for k in range(2):
-        for b in range(4):
-            rows = slice(b * 80, b * 80 + 80)
-            block = natural[k, rows].astype(F32)
-            for c in range(CACHE):
-                cache[k, c, rows] = block[:, c, :].astype(BF)
     swap.wait_recv()
     share.begin(2)
     for s in range(3):
@@ -379,21 +392,6 @@
     late(-1)
     late(1)
 
-    corner = lax.broadcasted_iota(jnp.int32, (WIDE, WIDE), 0) == lax.broadcasted_iota(
-        jnp.int32, (WIDE, WIDE), 1
-    )
-
-    def fold(f, carry):
-        for j in range(4):
-            i = j * 8 + f
-            gain = jnp.sum(jnp.where(corner, gain_row(gain_ref, i), 0.0), axis=1, keepdims=True)
-            folded[wide(f, WIDE), j * QKV : (j + 1) * QKV] = (
-                wqkv[wide(i, WIDE), :].astype(F32) * gain
-            ).astype(BF)
-        return carry
-
-    lax.fori_loop(0, 8, fold, 0)
-
     def arrived(*apart):
         for s in range(4):
             for d in apart:
@@ -475,6 +473,58 @@
     att[quarter] = mixed.astype(BF)
     att_in = [wire.send(att.at[quarter], att.at[quarter], who) for who in (here.xm, dg, here.cp)]
 
+    def lay(f, carry):
+        full1[f] = (
+            dot(near_hot[quarter], packed[f, 0:7].reshape(NEAR, WIDE))
+            + dot(rest_hot[quarter], packed[f, 7].reshape(REST, WIDE))
+        ).astype(BF)
+        return carry
+
+    lax.fori_loop(0, 8, lay, 0)
+    for copy in att_in + wo_in:
+        copy.wait_recv()
+
+    def spread(i, carry):
+        zz = lax.rem(z + ring_order(i), RING)
+        both = jnp.concatenate([att[q] for q in range(QUAD)], axis=1)
+        blocks = [woq[q, :, wide(zz, WIDE)] for q in range(QUAD)]
+        part2[zz] = dot(both, jnp.concatenate(blocks, axis=0)).astype(BF)
+        return carry
+
+    strips = [(lambda zz: zz, QUART * s, QUART, (UP, DOWN)[s % 2], None) for s in range(QUAD)]
+    ring = Ring(wire, here, part2, land2, strips)
+    spread(0, 0)
+    for s in range(QUAD):
+        ring.hop0(s)
+    lax.fori_loop(1, RING, spread, 0)
+    for k in (1, 2, 3):
+        for s in range(QUAD):
+            ring.hop(k, s)
+
+    def strip(s, d, first=0, n=QUART):
+        return full2.at[ring.zat(d), pl.ds(QUART * s + first, n)]
+
+    share = Share(
+        wire, here, lambda s, d, a, n: strip(s, d, 0, QUART), [(far, None) for _, _, _, far, _ in strips], 0
+    )
+    for s in range(QUAD):
+        rows = slice(QUART * s, QUART * s + QUART)
+        value = ring.total(s) + full1[z, rows].astype(F32)
+        full2[z, rows] = value.astype(BF)
+        share.begin(s)
+
+    def take(zz, first):
+        value = full2[zz].astype(F32)
+        scaled = (value * gain_row(final_ref, quarter * RING + zz)).astype(BF)
+        blocks = [wpq[q, wide(zz, WIDE), :] for q in range(QUAD)]
+        term = dot(scaled, jnp.concatenate(blocks, axis=1))
+        if first:
+            acc4[...] = term
+            squares[...] = value * value
+        else:
+            acc4[...] += term
+            squares[...] += value * value
+
     upper = (
         lax.broadcasted_iota(jnp.int32, (LANES, LANES), 0)
         <= lax.broadcasted_iota(jnp.int32, (LANES, LANES), 1)
@@ -491,58 +541,6 @@
         inside = ((row >= 0) & (row < OWN)).astype(F32)
         rank = dot(inside.astype(BF), upper)
         unpack[e] = jnp.where(rank - 1.0 == places, inside, 0.0).astype(BF)
-
-    def lay(f, carry):
-        full1[f] = (
-            dot(near_hot[quarter], packed[f, 0:7].reshape(NEAR, WIDE))
-            + dot(rest_hot[quarter], packed[f, 7].reshape(REST, WIDE))
-        ).astype(BF)
-        return carry
-
-    lax.fori_loop(0, 8, lay, 0)
-    for copy in att_in + wo_in:
-        copy.wait_recv()
-
-    def spread(i, carry):
-        zz = lax.rem(z + ring_order(i), RING)
-        both = jnp.concatenate([att[q] for q in range(QUAD)], axis=1)
-        blocks = [woq[q, :, wide(zz, WIDE)] for q in range(QUAD)]
-        part2[zz] = dot(both, jnp.concatenate(blocks, axis=0)).astype(BF)
-        return carry
-
-    strips = [(lambda zz: zz, QUART * s, QUART, (UP, DOWN)[s % 2], None) for s in range(QUAD)]
-    ring = Ring(wire, here, part2, land2, strips)
-    spread(0, 0)
-    for s in range(QUAD):
-        ring.hop0(s)
-    lax.fori_loop(1, RING, spread, 0)
-    for k in (1, 2, 3):
-        for s in range(QUAD):
-            ring.hop(k, s)
-
-    def strip(s, d, first=0, n=QUART):
-        return full2.at[ring.zat(d), pl.ds(QUART * s + first, n)]
-
-    share = Share(
-        wire, here, lambda s, d, a, n: strip(s, d, 0, QUART), [(far, None) for _, _, _, far, _ in strips], 0
-    )
-    for s in range(QUAD):
-        rows = slice(QUART * s, QUART * s + QUART)
-        value = ring.total(s) + full1[z, rows].astype(F32)
-        full2[z, rows] = value.astype(BF)
-        share.begin(s)
-
-    def take(zz, first):
-        value = full2[zz].astype(F32)
-        scaled = (value * gain_row(final_ref, quarter * RING + zz)).astype(BF)
-        blocks = [wpq[q, wide(zz, WIDE), :] for q in range(QUAD)]
-        term = dot(scaled, jnp.concatenate(blocks, axis=1))
-        if first:
-            acc4[...] = term
-            squares[...] = value * value
-        else:
-            acc4[...] += term
-            squares[...] += value * value
 
     for copy in wp_in:
         copy.wait_recv()
@@ -601,7 +599,7 @@
             unpack[e], outgo[e, away : away + CAP], (((0,), (0,)), ((), ())), preferred_element_type=F32
         )
     out_ref[...] = result[0:OWN].astype(BF)
-    flag_ref[...] = flag[0:8].astype(jnp.int32)
+    flag_ref[0, 0] = jnp.max(flag).astype(jnp.int32)
     for copy in wire.sent:
         copy.wait_send()
 
@@ -739,9 +737,9 @@
     hbm = pl.BlockSpec(memory_space=pl.ANY)
     out, flag = pl.pallas_call(
         kernel,
-        out_shape=[jax.ShapeDtypeStruct((OWN, HEAD), BF), jax.ShapeDtypeStruct((8, HEAD), jnp.int32)],
+        out_shape=[jax.ShapeDtypeStruct((OWN, HEAD), BF), jax.ShapeDtypeStruct((1, 1), jnp.int32)],
         in_specs=[vmem] * 5 + [hbm] * 6,
-        out_specs=[vmem, vmem],
+        out_specs=[vmem, pl.BlockSpec(memory_space=pltpu.SMEM)],
         scratch_shapes=[
             pltpu.VMEM((GROUPS, 16, LANES), jnp.int32),
             pltpu.VMEM((2, VOCAB_ROWS, CORE_SPAN), BF),

time: 108 us -> 107 us (level)
  local copies, waits for them, and re-layouts: 1.86 us -> 0.67 us
    slice x1 -> x0, local copies, waits for them, and re-layouts: 1.19 us -> none  [shards(): flag[0, 0] > 0]
where the time goes in v4:
time: 107 us
  Pallas kernels  105 us (98%)
    pallas_call x1, Pallas kernels, shards(): pl.pallas_call(kernel, out_shape=[jax.ShapeDtypeStruct((OWN, HEAD), BF),...  105 us

profile of v4, /device:TPU:1, one launch (start us, length us, event | category | flops | bytes accessed | tf_op | source)
XLA Modules:
  0.0 106.6 jit_solution(6558350226964562535)
XLA Ops:
  0.0 0.0 copy-start
  0.0 0.0 copy-start.4
  0.0 0.0 copy-start.5
  0.0 0.0 copy-start.6
  0.0 0.0 copy-start.7
  0.0 0.0 copy-start.8
  0.0 0.0 copy-start.9
  0.0 104.9 %shard_map.111 = (bf16[320,128]{1,0:T(8,128)(2,1)S(1)}, s32[1,1]{1,0:T(1,128)}) custom-call(s32[4,320]{1,0:T(4,128)} %bitcast.99, s32[320]{0:T(512)} %slots_ref.1, s32[320]{0:T(512)} %lens_ref.1, f32[64,128]{1,0:T(8,128)} %bitcast.93, f32[64,128]{1,0:T(8,128)} %bitcast.95, bf16[2,320,4,128]{3,2,1,0:T(4,128)(2,1)} %cache_ref.1, bf16[500,2048]{1,0:T(8,128)(2,1)} %table_ref.1, ...), custom_call_target="tpu_custom_call" | custom-call | tf_op jit(solution)/shard_map/pallas_call | solution.py:738
  105.7 0.0 copy-done
  105.7 0.0 copy-done.4
  105.7 0.0 copy-done.5
  105.7 0.0 copy-done.6
  105.7 0.0 copy-done.7
  105.7 0.0 copy-done.8
  105.7 0.0 copy-done.9
  105.7 0.3 conditional.1
  106.0 0.6 copy.57
Async XLA Ops:
  0.0 105.7 %copy-start = (bf16[500,2048]{1,0:T(8,128)(2,1)S(1)}, bf16[500,2048]{1,0:T(8,128)(2,1)}, u32[]{:S(2)}) copy-start(bf16[500,2048]{1,0:T(8,128)(2,1)} %table_ref.1) | copy-start | bytes 6144004
  0.0 105.7 %copy-start.4 = (f32[8192]{0:T(1024)S(1)}, f32[8192]{0:T(1024)}, u32[]{:S(2)}) copy-start(f32[8192]{0:T(1024)} %param.17) | copy-start | bytes 98308
  0.0 105.7 %copy-start.5 = (bf16[2,320,4,128]{3,2,1,0:T(4,128)(2,1)S(1)}, bf16[2,320,4,128]{3,2,1,0:T(4,128)(2,1)}, u32[]{:S(2)}) copy-start(bf16[2,320,4,128]{3,2,1,0:T(4,128)(2,1)} %cache_ref.1) | copy-start | bytes 1966084
  0.0 105.7 %copy-start.6 = (f32[8192]{0:T(1024)S(1)}, f32[8192]{0:T(1024)}, u32[]{:S(2)}) copy-start(f32[8192]{0:T(1024)} %param.22) | copy-start | bytes 98308
  0.0 105.7 %copy-start.7 = (s32[320,4]{0,1:T(4,128)S(1)}, s32[320,4]{0,1:T(4,128)}, u32[]{:S(2)}) copy-start(s32[320,4]{0,1:T(4,128)} %param.13) | copy-start | bytes 15364
  0.0 105.7 %copy-start.8 = (s32[320]{0:T(512)S(1)}, s32[320]{0:T(512)}, u32[]{:S(2)}) copy-start(s32[320]{0:T(512)} %slots_ref.1) | copy-start | bytes 3844
  0.0 105.7 %copy-start.9 = (s32[320]{0:T(512)S(1)}, s32[320]{0:T(512)}, u32[]{:S(2)}) copy-start(s32[320]{0:T(512)} %lens_ref.1) | copy-start | bytes 3844

commit v5 on v4

--- a/solution.py
+++ b/solution.py
@@ -392,6 +392,24 @@
     late(-1)
     late(1)
 
+    upper = (
+        lax.broadcasted_iota(jnp.int32, (LANES, LANES), 0)
+        <= lax.broadcasted_iota(jnp.int32, (LANES, LANES), 1)
+    ).astype(F32).astype(BF)
+    places = lax.broadcasted_iota(jnp.int32, (CAP, LANES), 0).astype(F32)
+    own_slots = info[g, 8:9, :]
+    for e in range(GROUPS):
+        row = info[e, 8:9, :] - g * OWN
+        inside = ((row >= 0) & (row < OWN)).astype(F32)
+        rank = dot(inside.astype(BF), upper)
+        pick = jnp.where(rank - 1.0 == places, inside, 0.0).astype(BF)
+        pack[e] = dot_lanes(pick, member[e]).astype(BF)
+        row = own_slots - e * OWN
+        inside = ((row >= 0) & (row < OWN)).astype(F32)
+        rank = dot(inside.astype(BF), upper)
+        unpack[e] = jnp.where(rank - 1.0 == places, inside, 0.0).astype(BF)
+
+
     def arrived(*apart):
         for s in range(4):
             for d in apart:
@@ -524,23 +542,6 @@
         else:
             acc4[...] += term
             squares[...] += value * value
-
-    upper = (
-        lax.broadcasted_iota(jnp.int32, (LANES, LANES), 0)
-        <= lax.broadcasted_iota(jnp.int32, (LANES, LANES), 1)
-    ).astype(F32).astype(BF)
-    places = lax.broadcasted_iota(jnp.int32, (CAP, LANES), 0).astype(F32)
-    own_slots = info[g, 8:9, :]
-    for e in range(GROUPS):
-        row = info[e, 8:9, :] - g * OWN
-        inside = ((row >= 0) & (row < OWN)).astype(F32)
-        rank = dot(inside.astype(BF), upper)
-        pick = jnp.where(rank - 1.0 == places, inside, 0.0).astype(BF)
-        pack[e] = dot_lanes(pick, member[e]).astype(BF)
-        row = own_slots - e * OWN
-        inside = ((row >= 0) & (row < OWN)).astype(F32)
-        rank = dot(inside.astype(BF), upper)
-        unpack[e] = jnp.where(rank - 1.0 == places, inside, 0.0).astype(BF)
 
     for copy in wp_in:
         copy.wait_recv()

time: 107 us -> 106 us (level)
  no operation moved by 1% of the time
where the time goes in v5:
time: 106 us
  Pallas kernels  104 us (98%)
    pallas_call x1, Pallas kernels, shards(): pl.pallas_call(kernel, out_shape=[jax.ShapeDtypeStruct((OWN, HEAD), BF),...  104 us

profile of v5, /device:TPU:1, one launch (start us, length us, event | category | flops | bytes accessed | tf_op | source)
XLA Modules:
  0.0 105.6 jit_solution(5726267749472468691)
XLA Ops:
  0.0 0.0 copy-start
  0.0 0.0 copy-start.4
  0.0 0.0 copy-start.5
  0.0 0.0 copy-start.6
  0.0 0.0 copy-start.7
  0.0 0.0 copy-start.8
  0.0 0.0 copy-start.9
  0.0 103.8 %shard_map.111 = (bf16[320,128]{1,0:T(8,128)(2,1)S(1)}, s32[1,1]{1,0:T(1,128)}) custom-call(s32[4,320]{1,0:T(4,128)} %bitcast.99, s32[320]{0:T(512)} %slots_ref.1, s32[320]{0:T(512)} %lens_ref.1, f32[64,128]{1,0:T(8,128)} %bitcast.93, f32[64,128]{1,0:T(8,128)} %bitcast.95, bf16[2,320,4,128]{3,2,1,0:T(4,128)(2,1)} %cache_ref.1, bf16[500,2048]{1,0:T(8,128)(2,1)} %table_ref.1, ...), custom_call_target="tpu_custom_call" | custom-call | tf_op jit(solution)/shard_map/pallas_call | solution.py:739
  104.6 0.0 copy-done
  104.6 0.0 copy-done.4
  104.6 0.0 copy-done.5
  104.6 0.0 copy-done.6
  104.6 0.0 copy-done.7
  104.6 0.0 copy-done.8
  104.6 0.0 copy-done.9
  104.7 0.3 conditional.1
  104.9 0.6 copy.57
Async XLA Ops:
  0.0 104.6 %copy-start = (bf16[500,2048]{1,0:T(8,128)(2,1)S(1)}, bf16[500,2048]{1,0:T(8,128)(2,1)}, u32[]{:S(2)}) copy-start(bf16[500,2048]{1,0:T(8,128)(2,1)} %table_ref.1) | copy-start | bytes 6144004
  0.0 104.6 %copy-start.4 = (f32[8192]{0:T(1024)S(1)}, f32[8192]{0:T(1024)}, u32[]{:S(2)}) copy-start(f32[8192]{0:T(1024)} %param.17) | copy-start | bytes 98308
  0.0 104.6 %copy-start.5 = (bf16[2,320,4,128]{3,2,1,0:T(4,128)(2,1)S(1)}, bf16[2,320,4,128]{3,2,1,0:T(4,128)(2,1)}, u32[]{:S(2)}) copy-start(bf16[2,320,4,128]{3,2,1,0:T(4,128)(2,1)} %cache_ref.1) | copy-start | bytes 1966084
  0.0 104.6 %copy-start.6 = (f32[8192]{0:T(1024)S(1)}, f32[8192]{0:T(1024)}, u32[]{:S(2)}) copy-start(f32[8192]{0:T(1024)} %param.22) | copy-start | bytes 98308
  0.0 104.6 %copy-start.7 = (s32[320,4]{0,1:T(4,128)S(1)}, s32[320,4]{0,1:T(4,128)}, u32[]{:S(2)}) copy-start(s32[320,4]{0,1:T(4,128)} %param.13) | copy-start | bytes 15364
  0.0 104.6 %copy-start.8 = (s32[320]{0:T(512)S(1)}, s32[320]{0:T(512)}, u32[]{:S(2)}) copy-start(s32[320]{0:T(512)} %slots_ref.1) | copy-start | bytes 3844
  0.0 104.6 %copy-start.9 = (s32[320]{0:T(512)S(1)}, s32[320]{0:T(512)}, u32[]{:S(2)}) copy-start(s32[320]{0:T(512)} %lens_ref.1) | copy-start | bytes 3844
